TPU v7x, 32 devices: a whole 2x2x4 slice. The times are simulated.
32 devices in a mesh: section: 2 (over core), dp: 4 (over y, x), tensor: 4 (over z).
Axes of the slice: x: 2, y: 2, z: 4, core: 2. Of those that a mesh axis runs over, the one named last changes fastest.
Arguments:
- images: bfloat16 [4, 3152, 768], P(None, ('dp', 'tensor')), may hold values from -6 to 6
- cotangent: bfloat16 [4, 3152, 768], P(None, ('dp', 'tensor')), may hold values from -6 to 6
- counts: int32 [4, 4], P(None, 'dp'), may hold values from 1 to 4, as said below
- ln1_gain: bfloat16 [2, 768], P('section', 'dp'), may hold values from 0.099609375 to 1.8984375
- ln1_bias: bfloat16 [2, 768], P('section', 'dp'), may hold values from -2 to 2
- q_bias: bfloat16 [2, 12, 64], P('section', 'tensor', 'dp'), may hold values from -3 to 3
- v_bias: bfloat16 [2, 12, 64], P('section', 'tensor', 'dp'), may hold values from -3 to 3
- qkv_weight: bfloat16 [2, 768, 3, 768], P('section', 'dp', None, 'tensor'), may hold values from -0.21875 to 0.21875
- out_weight: bfloat16 [2, 768, 768], P('section', 'tensor', 'dp'), may hold values from -0.875 to 0.875
- out_bias: bfloat16 [2, 768], P('section', 'dp'), may hold values from -2 to 2
- ln2_gain: bfloat16 [2, 768], P('section', 'dp'), may hold values from 0.099609375 to 1.8984375
- ln2_bias: bfloat16 [2, 768], P('section', 'dp'), may hold values from -2 to 2
- up_weight: bfloat16 [2, 768, 3072], P('section', 'dp', 'tensor'), may hold values from -0.21875 to 0.21875
- up_bias: bfloat16 [2, 48, 64], P('section', 'tensor', 'dp'), may hold values from -3 to 3
- down_weight: bfloat16 [2, 3072, 768], P('section', 'tensor', 'dp'), may hold values from -0.109375 to 0.109375
- down_bias: bfloat16 [2, 768], P('section', 'dp'), may hold values from -2 to 2
Outputs:
- section_out: bfloat16 [2, 4, 3152, 768], P('section', None, ('dp', 'tensor'))
- input_grad: bfloat16 [2, 4, 3152, 768], P('section', None, ('dp', 'tensor'))
- qkv_grad: float32 [2, 768, 3, 768], P('section', 'dp', None, 'tensor')
- out_weight_grad: float32 [2, 768, 768], P('section', 'tensor', 'dp')
- up_weight_grad: float32 [2, 768, 3072], P('section', 'dp', 'tensor')
- down_weight_grad: float32 [2, 3072, 768], P('section', 'tensor', 'dp')
- q_bias_grad: float32 [2, 12, 64], P('section', 'tensor', 'dp')
- v_bias_grad: float32 [2, 12, 64], P('section', 'tensor', 'dp')
- up_bias_grad: float32 [2, 48, 64], P('section', 'tensor', 'dp')
- vector_grad: float32 [2, 6, 768], P('section', None, ('dp', 'tensor'))
Inputs may be any that keep to these rules, and one draw needn't show every extreme that they name: counts[m, i] live image slots of dp index i in micro-batch m are its first ones; in every micro-batch some index has all 4 live.
All inputs are finite; a program needn't handle non-finite values.
Results may differ from a plain program's by a relative error of at most 0.017.
Values may be sent and summed in bfloat16 or wider, within the bound.
A program may use at most 256 MiB of HBM per device.

v0:
```python
import functools
import jax
import jax.numpy as jnp
from jax import lax
from jax.experimental import pallas as pl
from jax.experimental.pallas import tpu as pltpu
from jax.sharding import PartitionSpec as P

CHUNK_ROWS = 48
BLOCK_TICKS = 3
PAUSE = 0
SMALL_TICKS = 2
GLAGS = [0, 2, 4, 5, 8, 9, 12, 14]
MESH_ID = pl.DeviceIdType.MESH


def slot_sizes(n_dp, n_tensor):
    bits = [b for b in range(n_dp.bit_length()) if (1 << b) < n_dp]
    mid = n_tensor // 2
    weights = [bin(e).count("1") for e in range(n_dp)]

    def plane(weight):
        total = 0
        for j in range(mid):
            for e in range(n_dp):
                if weights[e] == weight:
                    for b in bits:
                        if not e >> b & 1:
                            chosen = [c for c in bits if (e | 1 << b) >> c & 1]
                            total += chosen[j % len(chosen)] == b
                    total += 2 * (weight >= 2) + 1
        return total

    first = [2 + len(bits)]
    columns = [2 * (2 + len(bits))] * (n_tensor - 1)
    planes = [plane(w) for w in range(1, len(bits) + 1)]
    crossed = [3 * mid * sum(w >= 2 for w in weights)]
    rest = [mid * sum(w == 1 for w in weights)]
    return first + [columns[0], planes[0], columns[1]] + planes[1:] + columns[2:] + crossed + rest


class Place:
    def __init__(self, n_dp, n_tensor):
        self.n_dp, self.n_tensor = n_dp, n_tensor
        self.mid = n_tensor // 2
        self.bits = [b for b in range(n_dp.bit_length()) if (1 << b) < n_dp]
        self.s = lax.axis_index("section")
        self.d = lax.axis_index("dp")
        self.t = lax.axis_index("tensor")
        self.upper = lax.div(self.t, self.mid)
        self.has_next = self.t < n_tensor - 1
        self.has_prev = self.t > 0

    def away(self, e):
        other = self.d
        for b in self.bits:
            if e >> b & 1:
                other = other + (1 << b) * (1 - 2 * lax.rem(lax.div(self.d, 1 << b), 2))
        return other

    def last_bit(self, e, j):
        chosen = [b for b in self.bits if e >> b & 1]
        return chosen[j % len(chosen)]

    def own_side(self, j):
        return self.upper * self.mid + j

    def other_side(self, j):
        return (1 - self.upper) * self.mid + j

    def sibling(self):
        return (1 - self.s, self.d, self.t)

    def along(self, step):
        return (self.s, self.d, self.t + step)

    def hop(self, b):
        return (self.s, self.away(1 << b), self.t)

    def meet(self):
        barrier = pltpu.get_barrier_semaphore()
        line = [(self.s, self.d, lax.rem(self.t + k, self.n_tensor)) for k in range(1, self.n_tensor)]
        others = [self.sibling()] + [self.hop(b) for b in self.bits] + line
        for device in others:
            pl.semaphore_signal(barrier, inc=1, device_id=device, device_id_type=MESH_ID)
        pl.semaphore_wait(barrier, len(others))

    def rows_away(self, source, target, sec, sems):
        return pltpu.make_async_remote_copy(
            src_ref=source.at[sec],
            dst_ref=target.at[self.s],
            send_sem=sems.at[1],
            recv_sem=sems.at[2],
            device_id=self.sibling(),
            device_id_type=MESH_ID,
        )

    def hand_out(self, source, target, sec, sems):
        @pl.when(sec == self.s)
        def _():
            pltpu.make_async_copy(source.at[sec], target.at[self.s], sems.at[0]).start()

        @pl.when(sec != self.s)
        def _():
            self.rows_away(source, target, sec, sems).start()

    def handed_out(self, source, target, sems):
        pltpu.make_async_copy(source.at[0], target.at[self.s], sems.at[0]).wait()
        self.rows_away(source, target, 0, sems).wait()

    def by_weight(self, weight):
        return [e for e in range(self.n_dp) if bin(e).count("1") == weight]


DH = 64
SEQ = 197
EPS = 1e-06
F32 = jnp.float32
BF16 = jnp.bfloat16
ROWS = 208


def dot(left, right):
    return jnp.dot(left, right, preferred_element_type=F32)


def dot_cols(left, right):
    return lax.dot_general(left, right, (((1,), (1,)), ((), ())), preferred_element_type=F32)


def unit_rows(values):
    average = jnp.mean(values, axis=-1, keepdims=True)
    centered = values - average
    scale = lax.rsqrt(jnp.mean(centered * centered, axis=-1, keepdims=True) + EPS)
    return centered * scale, scale


def unit_rows_back(grad_unit, unit, scale):
    along = jnp.mean(grad_unit * unit, axis=-1, keepdims=True)
    return scale * (grad_unit - jnp.mean(grad_unit, axis=-1, keepdims=True) - unit * along)


def gelu_parts(hidden):
    below = 0.5 * (1.0 + lax.erf(hidden * (0.5**0.5)))
    density = jnp.exp(-0.5 * hidden * hidden) * 0.3989422804014327
    return hidden * below, below + hidden * density


def forward_kernel(n_dp, n_tensor, images, *refs):
    (
        shard, rows, live, *given,
        out, sec_rows, row_out, qkv_out, p_out, heads_out, middle_out, active_out, slope_out, vec,
        w_buf, qkv_st, p_st, heads_st, active_st, slope_st, middle_st, normed, acc, row_buf,
        qkv_bias, up_bias, vec_in, qkv_bias_in, up_bias_in,
        own_sem, recv_sem, send_sem, part_sem, load_sem, store_sem, active_sem, once_sem, row_sem, small_sem,
    ) = refs
    at = Place(n_dp, n_tensor)
    n_section = out.shape[0]
    n_blk, depth, span = shard.shape
    half = span // 2
    n_all = n_section * n_blk
    part = vec.shape[2] // n_tensor
    n_heads = part // DH

    def spread(value):
        return jnp.concatenate([jnp.where(at.d == k, value, 0.0) for k in range(n_dp)], axis=1)

    def spread_heads(ref):
        values = ref[0].astype(F32)
        return jnp.concatenate([spread(values[h : h + 1]) for h in range(values.shape[0])], axis=1)

    vec[...] = jnp.zeros_like(vec)
    qkv_bias[...] = jnp.zeros_like(qkv_bias)
    up_bias[...] = jnp.zeros_like(up_bias)
    placed = jnp.concatenate([spread(ref[...].astype(F32)) for ref in given[:6]], axis=0)
    vec[at.s] = jnp.where(at.t == 0, placed, 0.0)
    q_row, v_row = spread_heads(given[6]), spread_heads(given[7])
    qkv_bias[at.s, at.t] = jnp.concatenate([q_row, jnp.zeros_like(q_row), v_row], axis=1)
    up_bias[at.s, at.t] = spread_heads(given[8])
    at.meet()

    def whole(sec, b):
        return out.at[sec, b, at.t, rows_of(0), :]

    def rows_of(e):
        return pl.ds(pl.multiple_of(at.away(e) * depth, 16), depth)

    lanes = pl.ds(pl.multiple_of(at.s * half, 128), half)

    def piece(i, e, tt):
        return out.at[lax.div(i, n_blk), lax.rem(i, n_blk), tt, rows_of(e), lanes]

    def share(b):
        return pltpu.make_async_remote_copy(
            src_ref=shard.at[b],
            dst_ref=whole(at.s, b),
            send_sem=own_sem.at[1, b],
            recv_sem=own_sem.at[2, b],
            device_id=at.sibling(),
            device_id_type=MESH_ID,
        )

    for b in range(n_blk):
        pltpu.make_async_copy(shard.at[b], whole(at.s, b), own_sem.at[0, b]).start()
        share(b).start()

    def push(i, e, tt, device, e_there, slot, start):
        copy = pltpu.make_async_remote_copy(
            src_ref=piece(i, e, tt),
            dst_ref=piece(i, e, tt),
            send_sem=send_sem.at[i, slot],
            recv_sem=recv_sem.at[i, e_there * n_tensor + tt],
            device_id=device,
            device_id_type=MESH_ID,
        )
        if start:
            copy.start()
        else:
            copy.wait_send()

    def push_sib(i, e, tt, slot, start):
        copy = pltpu.make_async_remote_copy(
            src_ref=piece(i, e, tt),
            dst_ref=piece(i, e, tt),
            send_sem=send_sem.at[i, slot],
            recv_sem=part_sem.at[i, 0 if e == 0 else 1],
            device_id=at.sibling(),
            device_id_type=MESH_ID,
        )
        if start:
            copy.start()
        else:
            copy.wait_send()

    def await_piece(i, e, tt):
        pltpu.make_async_remote_copy(
            src_ref=piece(i, e, tt),
            dst_ref=piece(i, e, tt),
            send_sem=send_sem.at[i, 0],
            recv_sem=recv_sem.at[i, e * n_tensor + tt],
            device_id=at.sibling(),
            device_id_type=MESH_ID,
        ).wait_recv()

    def steps(i, start):
        slots = iter(range(10_000))

        def maybe(cond, action):
            if cond is None:
                action()
            else:
                pl.when(cond)(action)

        def ready(e, tt, cond=None):
            if start:
                maybe(cond, lambda: await_piece(i, e, tt))

        def go(e, tt, device, e_there, cond=None):
            slot = next(slots)
            maybe(cond, lambda: push(i, e, tt, device, e_there, slot, start))

        def go_sib(e, tt, cond=None):
            slot = next(slots)
            maybe(cond, lambda: push_sib(i, e, tt, slot, start))

        def first():
            sec, b = lax.div(i, n_blk), lax.rem(i, n_blk)
            if start:

                @pl.when(sec == at.s)
                def _():
                    pltpu.make_async_copy(shard.at[b], whole(at.s, b), own_sem.at[0, b]).wait()

                @pl.when(sec != at.s)
                def _():
                    pltpu.make_async_remote_copy(
                        src_ref=shard.at[b],
                        dst_ref=whole(1 - at.s, b),
                        send_sem=own_sem.at[1, b],
                        recv_sem=own_sem.at[2, b],
                        device_id=at.sibling(),
                        device_id_type=MESH_ID,
                    ).wait_recv()

            go(0, at.t, at.along(1), 0, at.has_next)
            go(0, at.t, at.along(-1), 0, at.has_prev)
            for b in at.bits:
                go(0, at.t, at.hop(b), 1 << b)

        def column(k):
            low, high = at.t >= k, at.t + k < n_tensor
            for tt, cond, dev, more in (
                (at.t - k, low, at.along(1), jnp.logical_and(low, at.has_next)),
                (at.t + k, high, at.along(-1), jnp.logical_and(high, at.has_prev)),
            ):
                ready(0, tt, cond)
                go(0, tt, dev, 0, more)
                for b in at.bits:
                    go(0, tt, at.hop(b), 1 << b, cond)
                go_sib(0, tt, cond)

        def plane(weight):
            for j in range(at.mid):
                for e in at.by_weight(weight):
                    tt = at.own_side(j)
                    ready(e, tt)
                    for b in at.bits:
                        if not e >> b & 1 and at.last_bit(e | 1 << b, j) == b:
                            go(e, tt, at.hop(b), e | 1 << b)
                    if weight >= 2:
                        go(e, tt, at.along(1), e, at.t == at.mid - 1)
                        go(e, tt, at.along(-1), e, at.t == at.mid)
                    go_sib(e, tt)

        def crossed():
            for weight in range(2, len(at.bits) + 1):
                for e in at.by_weight(weight):
                    for j in range(at.mid):
                        tt = at.other_side(j)
                        ready(e, tt)
                        up = jnp.logical_and(at.t >= at.mid, at.has_next)
                        down = jnp.logical_and(at.t < at.mid, at.has_prev)
                        go(e, tt, at.along(1), e, up)
                        go(e, tt, at.along(-1), e, down)
                        go_sib(e, tt)

        def rest():
            for e in at.by_weight(1):
                for j in range(at.mid):
                    tt = at.other_side(j)
                    ready(e, tt)
                    go_sib(e, tt)

        groups = [first]
        for k in range(1, n_tensor):
            groups.append(functools.partial(column, k))
        planes = [functools.partial(plane, w) for w in range(1, len(at.bits) + 1)]
        merged = [groups[0]]
        order = [groups[1], planes[0], groups[2]] + planes[1:] + groups[3:] + [crossed, rest]
        return merged + order, slots


    small = [(vec, vec_in), (qkv_bias, qkv_bias_in), (up_bias, up_bias_in)]
    n_hops = len(at.bits)

    def small_copies(device, slot, to_place):
        return [
            pltpu.make_async_remote_copy(
                src_ref=mine.at[at.s],
                dst_ref=mine.at[at.s] if to_place else came_in.at[slot],
                send_sem=small_sem.at[0, slot, n],
                recv_sem=small_sem.at[1, slot, n],
                device_id=device,
                device_id_type=MESH_ID,
            )
            for n, (mine, came_in) in enumerate(small)
        ]

    def small_send(stage):
        if stage < n_hops:
            return [small_copies(at.hop(stage), stage, False)]
        if stage == n_hops:
            other = [lax.rem(at.t + k, n_tensor) for k in range(1, n_tensor)]
            return [small_copies((at.s, at.d, tt), n_hops + k, False) for k, tt in enumerate(other)]
        return [small_copies(at.sibling(), n_hops + n_tensor - 1, True)]

    def small_take(stage):
        sent = small_send(stage)
        for copies in sent:
            for copy in copies:
                copy.wait()
        if stage <= n_hops:
            for mine, came_in in small:
                total = mine[at.s]
                for slot in range(stage, stage + len(sent)):
                    total = total + came_in[slot]
                mine[at.s] = total

    def small_step(tick):
        for stage in range(n_hops + 3):

            @pl.when(tick == 1 + 2 * stage)
            def _():
                if stage:
                    small_take(stage - 1)
                if stage < n_hops + 2:
                    for copies in small_send(stage):
                        for copy in copies:
                            copy.start()

    def load(i, k, par):
        return pltpu.make_async_copy(out.at[i // n_blk, i % n_blk, k], w_buf.at[par], load_sem.at[par])

    def stores(i, k, par):
        sec, b = i // n_blk, i % n_blk
        if b == 0:
            pairs = [
                (qkv_st.at[par], qkv_out.at[sec, k], store_sem.at[par, 0]),
                (p_st.at[par], p_out.at[sec, k], store_sem.at[par, 1]),
                (heads_st.at[par], heads_out.at[sec, k], store_sem.at[par, 2]),
            ]
        elif b == 1:
            pairs = [(slope_st.at[par], slope_out.at[sec, k], store_sem.at[par, 3])]
        else:
            pairs = []
        return [pltpu.make_async_copy(*pair) for pair in pairs]

    def store_active(sec, k):
        return pltpu.make_async_copy(active_st.at[k], active_out.at[sec, k], active_sem.at[k])

    def store_middle(sec):
        return pltpu.make_async_copy(middle_st, middle_out.at[sec], once_sem.at[0])

    def store_rows(sec):
        return pltpu.make_async_copy(row_buf.at[sec], row_out.at[sec], once_sem.at[1 + sec])

    def attn_step(sec, k, par):
        @pl.when(k == 0)
        def _():
            values = (rows if sec == 0 else row_buf.at[sec - 1])[...].astype(F32)
            unit, _ = unit_rows(values)
            normed[...] = (unit * vec[sec, 0:1] + vec[sec, 1:2]).astype(BF16)
            acc[...] = values + vec[sec, 2:3]

        mixed = (dot(normed[...], w_buf[par, :, : 3 * part]) + qkv_bias[sec, k]).astype(BF16)
        qkv_st[par] = mixed
        keep = lax.broadcasted_iota(jnp.int32, (ROWS, ROWS), 0) < SEQ
        per_image = []
        for image in range(images):
            here = mixed[image * ROWS : (image + 1) * ROWS]
            per_head = []
            for head in range(n_heads):
                q, key, v = (
                    here[:, c * part + head * DH : c * part + (head + 1) * DH] for c in range(3)
                )
                scores = jnp.where(keep, dot_cols(key, q) * DH**-0.5, -1e30)
                scores = jnp.exp(scores - jnp.max(scores, axis=0, keepdims=True))
                total = jnp.sum(scores, axis=0, keepdims=True)
                chances = (scores * (1.0 / total)).astype(BF16)
                p_st[par, image, head] = chances
                per_head.append(dot(v.T, chances).T.astype(BF16))
            per_image.append(jnp.concatenate(per_head, axis=1))
        heads = jnp.concatenate(per_image, axis=0)
        heads_st[par] = heads
        acc[...] += dot_cols(heads, w_buf[par, :, 3 * part :])

    def up_step(sec, k, par):
        @pl.when(k == 0)
        def _():
            if sec:
                store_middle(sec - 1).wait()
            middle = acc[...]
            middle_st[...] = middle
            unit, _ = unit_rows(middle)
            normed[...] = (unit * vec[sec, 3:4] + vec[sec, 4:5]).astype(BF16)
            acc[...] = middle + vec[sec, 5:6]
            store_middle(sec).start()

        if sec:
            store_active(sec - 1, k).wait()
        hidden = dot(normed[...], w_buf[par]) + up_bias[sec, k]
        active, slope = gelu_parts(hidden)
        active_st[k] = active.astype(BF16)
        slope_st[par] = slope.astype(BF16)
        store_active(sec, k).start()

    def down_step(sec, k, par):
        acc[...] += dot_cols(active_st[k], w_buf[par])

        @pl.when(k == n_tensor - 1)
        def _():
            row_buf[sec] = (acc[...] * live[...]).astype(BF16)
            store_rows(sec).start()
            at.hand_out(row_buf, sec_rows, sec, row_sem)

    def compute(i, k):
        sec, b = i // n_blk, i % n_blk
        par = lax.rem(k, 2)

        @pl.when(k == 0)
        def _():
            for group, ref in (
                (0, out.at[sec, b, pl.ds(0, n_tensor - 1), pl.ds(0, depth), pl.ds(0, half)]),
                (1, out.at[sec, b, :, pl.ds(0, (n_dp - 1) * depth), pl.ds(0, half)]),
            ):
                pltpu.make_async_copy(ref, ref, part_sem.at[i, group]).wait()
            load(i, 0, 0).start()
            if sec and b < 2:
                for back in (n_tensor - 2, n_tensor - 1):
                    for copy in stores(i - n_blk, back, back % 2):
                        copy.wait()

        load(i, k, par).wait()

        @pl.when(k < n_tensor - 1)
        def _():
            load(i, k + 1, 1 - par).start()

        if b < 2:

            @pl.when(k >= 2)
            def _():
                for copy in stores(i, k - 2, par):
                    copy.wait()

        (attn_step, up_step, down_step)[b](sec, k, par)
        for copy in stores(i, k, par):
            copy.start()

    lags = gather_lags(len(slot_sizes(n_dp, n_tensor)))
    base = max(lags) + 1

    def body(it, carry):
        for g, lag in sorted(enumerate(lags), key=lambda item: item[1]):
            i = lax.div(it - lag, n_tensor)

            @pl.when(jnp.logical_and(it - lag == i * n_tensor, jnp.logical_and(it >= lag, i < n_all)))
            def _():
                run_group(i, g)

        small_step(it)
        for i in range(n_all):
            first = base + i * n_tensor

            @pl.when(jnp.logical_and(it >= first, it < first + n_tensor))
            def _():
                compute(i, it - first)

        return carry

    def run_group(i, g):
        groups, slots = steps(i, True)
        for _ in range(sum(slot_sizes(n_dp, n_tensor)[:g])):
            next(slots)
        groups[g]()

    lax.fori_loop(0, base + n_all * n_tensor, body, 0)

    def finish(i, carry):
        groups, _ = steps(i, False)
        for g in groups:
            g()
        return carry

    lax.fori_loop(0, n_all, finish, 0)
    for b in range(n_blk):
        share(b).wait_send()
    last = n_section - 1
    for b in range(2):
        for back in (n_tensor - 2, n_tensor - 1):
            for copy in stores(last * n_blk + b, back, back % 2):
                copy.wait()
    for k in range(n_tensor):
        store_active(last, k).wait()
    store_middle(last).wait()
    for sec in range(n_section):
        store_rows(sec).wait()
    at.handed_out(row_buf, sec_rows, row_sem)


def gather_lags(n_groups):
    return GLAGS


def gather_and_forward(shard, rows, live, given, n_section, n_dp, n_tensor):
    n_blk, depth, span = shard.shape
    n_rows, width = rows.shape
    images = n_rows // ROWS
    part = width // n_tensor
    n_heads = part // DH
    n_all = n_section * n_blk
    n_hops = n_dp.bit_length() - 1
    n_sends = sum(slot_sizes(n_dp, n_tensor))
    n_small = n_hops + n_tensor
    shape = jax.ShapeDtypeStruct
    hbm = pl.BlockSpec(memory_space=pl.ANY)
    vmem = pl.BlockSpec(memory_space=pltpu.VMEM)
    dma = pltpu.SemaphoreType.DMA
    return pl.pallas_call(
        functools.partial(forward_kernel, n_dp, n_tensor, images),
        out_shape=[
            shape((n_section, n_blk, n_tensor, width, span), BF16),
            shape((n_section, n_rows, width), BF16),
            shape((n_section, n_rows, width), BF16),
            shape((n_section, n_tensor, n_rows, 3 * part), BF16),
            shape((n_section, n_tensor, images, n_heads, ROWS, ROWS), BF16),
            shape((n_section, n_tensor, n_rows, part), BF16),
            shape((n_section, n_rows, width), F32),
            shape((n_section, n_tensor, n_rows, span), BF16),
            shape((n_section, n_tensor, n_rows, span), BF16),
            shape((n_section, 6, width), F32),
        ],
        in_specs=[hbm] + [vmem] * (2 + len(given)),
        out_specs=[hbm] * 9 + [vmem],
        scratch_shapes=[
            pltpu.VMEM((2, width, span), BF16),
            pltpu.VMEM((2, n_rows, 3 * part), BF16),
            pltpu.VMEM((2, images, n_heads, ROWS, ROWS), BF16),
            pltpu.VMEM((2, n_rows, part), BF16),
            pltpu.VMEM((n_tensor, n_rows, span), BF16),
            pltpu.VMEM((2, n_rows, span), BF16),
            pltpu.VMEM((n_rows, width), F32),
            pltpu.VMEM((n_rows, width), BF16),
            pltpu.VMEM((n_rows, width), F32),
            pltpu.VMEM((n_section, n_rows, width), BF16),
            pltpu.VMEM((n_section, n_tensor, 1, 3 * part), F32),
            pltpu.VMEM((n_section, n_tensor, 1, span), F32),
            pltpu.VMEM((n_small, 6, width), F32),
            pltpu.VMEM((n_small, n_tensor, 1, 3 * part), F32),
            pltpu.VMEM((n_small, n_tensor, 1, span), F32),
            dma((3, n_blk)),
            dma((n_all, n_dp * n_tensor)),
            dma((n_all, n_sends)),
            dma((n_all, 2)),
            dma((2,)),
            dma((2, 4)),
            dma((n_tensor,)),
            dma((1 + n_section,)),
            dma((3,)),
            dma((2, n_small, 3)),
        ],
        compiler_params=pltpu.CompilerParams(
            collective_id=0, has_side_effects=True, vmem_limit_bytes=56 * 1024 * 1024
        ),
    )(shard, rows, live, *given)


class Slots:
    def __init__(self, n_dp, n_tensor):
        self.n_tensor = n_tensor
        bits = [b for b in range(n_dp.bit_length()) if (1 << b) < n_dp]
        mid = n_tensor // 2
        count = len(bits) * n_tensor
        self.line = count
        count += n_tensor + 1
        self.hops = {}
        self.cross = {}
        for e in range(1, n_dp):
            if bin(e).count("1") >= 2:
                self.cross[e] = count
                count += n_tensor
            for j in range(mid):
                for b in bits:
                    if not e >> b & 1:
                        chosen = [c for c in bits if (e | 1 << b) >> c & 1]
                        if chosen[j % len(chosen)] == b:
                            self.hops[e, j, b] = count
                            count += 1
        self.count = count


def reduce_lags(n_groups):
    return [0, 0] + [2 + 3 * min(g, 2) + 2 * max(g - 2, 0) for g in range(n_groups - 2)]


def backward_kernel(
    n_dp, n_tensor, images, weights, cotangent, live, vec, *refs
):
    first_rows, row_out, *saved = refs[:8]
    (
        out, sec_grads, d_vec, d_qkv_bias, d_up_bias,
        own, came, final, vec_in, qkv_bias_in, up_bias_in, ring, stage, w_buf, hidden_buf, qkv_buf, p_buf, heads_buf, rows_buf, middle_buf,
        grad_out, grad_low, left_t, right_t, acc, grad_mid,
        load_sem, stage_sem, credit, recv_sem, send_sem, out_sem, small_sem, row_sem,
    ) = refs[8:]
    at = Place(n_dp, n_tensor)
    slots = Slots(n_dp, n_tensor)
    n_section, n_blk = weights.shape[:2]
    n_all = n_section * n_blk
    depth, half = final.shape[1:]
    part = vec.shape[2] // n_tensor
    n_heads = part // DH
    lanes = pl.ds(pl.multiple_of(at.s * half, 128), half)
    sizes = send_sizes(n_dp, n_tensor)
    at.meet()

    def place(i):
        return n_section - 1 - lax.div(i, n_blk), n_blk - 1 - lax.rem(i, n_blk)

    def steps(i, start):
        counter = iter(range(10_000))

        def rows(e):
            return pl.multiple_of(at.away(e) * depth, 16)

        def piece(e, tt):
            return own.at[i, tt, pl.ds(rows(e), depth), :]

        def maybe(cond, action):
            if cond is None:
                action()
            else:
                pl.when(cond)(action)

        def remote(e, tt, device, slot):
            k = next(counter)
            return pltpu.make_async_remote_copy(
                src_ref=piece(e, tt),
                dst_ref=came.at[i, slot],
                send_sem=send_sem.at[i, k],
                recv_sem=recv_sem.at[i, slot],
                device_id=device,
                device_id_type=MESH_ID,
            )

        def send(e, tt, device, slot, cond=None):
            copy = remote(e, tt, device, slot)
            maybe(cond, copy.start if start else copy.wait_send)

        def arrive(slot, cond=None):
            if start:
                copy = pltpu.make_async_copy(came.at[i, slot], came.at[i, slot], recv_sem.at[i, slot])
                maybe(cond, copy.wait)

        def total(e, tt, arrived, target=None):
            if not start or (target is None and not arrived):
                return
            base = rows(e)

            def chunk(c, carry):
                here = pl.ds(pl.multiple_of(base + c * CHUNK_ROWS, 16), CHUNK_ROWS)
                local = pl.ds(pl.multiple_of(c * CHUNK_ROWS, 16), CHUNK_ROWS)
                acc = own[i, tt, here, :].astype(jnp.float32)
                for slot in arrived:
                    acc = acc + came[i, slot, local, :].astype(jnp.float32)
                if target is None:
                    own[i, tt, here, :] = acc.astype(own.dtype)
                else:
                    target[i, local, :] = acc
                return carry

            lax.fori_loop(0, depth // CHUNK_ROWS, chunk, 0)

        def more(e, tt, slot, target=None):
            base = rows(e)

            def chunk(c, carry):
                here = pl.ds(pl.multiple_of(base + c * CHUNK_ROWS, 16), CHUNK_ROWS)
                local = pl.ds(pl.multiple_of(c * CHUNK_ROWS, 16), CHUNK_ROWS)
                acc = came[i, slot, local, :].astype(jnp.float32)
                if target is None:
                    own[i, tt, here, :] = (own[i, tt, here, :].astype(jnp.float32) + acc).astype(own.dtype)
                else:
                    target[i, local, :] = target[i, local, :] + acc
                return carry

            lax.fori_loop(0, depth // CHUNK_ROWS, chunk, 0)

        def also(e, tt, slot, cond, target=None):
            if start:

                def add():
                    arrive(slot)
                    more(e, tt, slot, target)

                pl.when(cond)(add)

        def line_slot(tt, from_next):
            return slots.line + tt + (0 if from_next else 1)

        def crossing():
            for e in range(1, n_dp):
                if bin(e).count("1") >= 2:
                    for j in range(at.mid):
                        tt = at.other_side(j)
                        slot = slots.cross[e] + tt
                        total(e, tt, [])
                        is_upper = at.t >= at.mid
                        also(e, tt, slot, jnp.logical_and(is_upper, at.has_next))
                        also(e, tt, slot, jnp.logical_and(jnp.logical_not(is_upper), at.has_prev))
                        send(e, tt, at.along(-1), slot, is_upper)
                        send(e, tt, at.along(1), slot, jnp.logical_not(is_upper))

        def leaves():
            for j in range(at.mid):
                for e in at.by_weight(1):
                    tt = at.other_side(j)
                    b = at.last_bit(e, j)
                    total(e, tt, [])
                    send(e, tt, at.hop(b), b * n_tensor + tt)

        def plane(weight):
            for e in at.by_weight(weight):
                for j in range(at.mid):
                    tt = at.own_side(j)
                    b = at.last_bit(e, j)
                    arrived = [slots.hops[e, j, c] for c in at.bits if (e, j, c) in slots.hops]
                    for slot in arrived:
                        arrive(slot)
                    total(e, tt, arrived)
                    if weight >= 2:
                        slot = slots.cross[e] + tt
                        also(e, tt, slot, at.t == at.mid - 1)
                        also(e, tt, slot, at.t == at.mid)
                    rest = e & ~(1 << b)
                    there = b * n_tensor + tt if rest == 0 else slots.hops[rest, j, b]
                    send(e, tt, at.hop(b), there)

        def column(k):
            low, high = at.t >= k, at.t + k < n_tensor
            for tt, cond, step, chain, from_next in (
                (at.t - k, low, -1, jnp.logical_and(low, at.has_next), True),
                (at.t + k, high, 1, jnp.logical_and(high, at.has_prev), False),
            ):
                arrived = [b * n_tensor + tt for b in at.bits]

                def sums(tt=tt, arrived=arrived):
                    for slot in arrived:
                        arrive(slot)
                    total(0, tt, arrived)

                if start:
                    pl.when(cond)(sums)
                slot = line_slot(tt, from_next)
                also(0, tt, slot, chain)
                send(0, tt, at.along(step), slot, cond)

        def last():
            arrived = [b * n_tensor + at.t for b in at.bits]
            for slot in arrived:
                arrive(slot)
            total(0, at.t, arrived, final)
            also(0, at.t, line_slot(at.t, True), at.has_next, final)
            also(0, at.t, line_slot(at.t, False), at.has_prev, final)
            sec, b = place(i)
            stay = pltpu.make_async_copy(final.at[i], out.at[b, :, lanes], out_sem.at[0, i])
            go = pltpu.make_async_remote_copy(
                src_ref=final.at[i],
                dst_ref=out.at[b, :, lanes],
                send_sem=out_sem.at[1, i],
                recv_sem=out_sem.at[2, i],
                device_id=at.sibling(),
                device_id_type=MESH_ID,
            )

            @pl.when(sec == at.s)
            def _():
                if start:
                    stay.start()
                else:
                    stay.wait()

            @pl.when(sec != at.s)
            def _():
                if start:
                    go.start()
                else:
                    go.wait_send()

        groups = [crossing, leaves]
        groups += [functools.partial(plane, w) for w in range(len(at.bits), 0, -1)]
        groups += [functools.partial(column, k) for k in range(n_tensor - 1, 0, -1)] + [last]
        return groups, counter

    lags = reduce_lags(len(sizes))

    def run_group(i, g):
        groups, counter = steps(i, True)
        for _ in range(sum(sizes[:g])):
            next(counter)
        groups[g]()

    phases = [(kind, sec) for sec in range(n_section - 1, -1, -1) for kind in ("ffn", "attn")]

    def loads(phase, k, par):
        kind, sec = phases[phase]
        rows = first_rows if sec == 0 else row_out.at[sec - 1]
        qkv, p, heads, middle, active, slope = (ref.at[sec] for ref in saved)
        if kind == "ffn":
            pairs = [
                (weights.at[sec, 1, k], w_buf.at[par, 0]),
                (weights.at[sec, 2, k], w_buf.at[par, 1]),
                (active.at[k], hidden_buf.at[par, 0]),
                (slope.at[k], hidden_buf.at[par, 1]),
            ]
            once = (middle, middle_buf)
        else:
            pairs = [
                (weights.at[sec, 0, k], w_buf.at[par, 0]),
                (qkv.at[k], qkv_buf.at[par]),
                (p.at[k], p_buf.at[par]),
                (heads.at[k], heads_buf.at[par]),
            ]
            once = (rows, rows_buf)
        copies = [
            pltpu.make_async_copy(src, dst, load_sem.at[par, n]) for n, (src, dst) in enumerate(pairs)
        ]
        return copies, lambda: pltpu.make_async_copy(*once, load_sem.at[0, 4])

    def start_loads(phase, k, par, is_first):
        copies, once = loads(phase, k, par)
        for copy in copies:
            copy.start()
        if is_first:
            once().start()

    def blocks_of(phase):
        kind, sec = phases[phase]
        base = (n_section - 1 - sec) * n_blk
        return [base, base + 1] if kind == "ffn" else [base + 2]

    def shared(par, q):
        return pltpu.make_async_remote_copy(
            src_ref=stage.at[par, q],
            dst_ref=ring.at[par, q],
            send_sem=stage_sem.at[0, par, q],
            recv_sem=stage_sem.at[1, par, q],
            device_id=at.sibling(),
            device_id_type=MESH_ID,
        )

    def before_emit(phase, k, par):
        if phase == 0:

            @pl.when(k >= 2)
            def _():
                for q in range(2):
                    shared(par, q).wait_send()
                pl.semaphore_wait(credit.at[par], 1)

        else:
            same, back = len(blocks_of(phase)), len(blocks_of(phase - 1))
            for q in range(max(same, back)):
                if q < same and q < back:
                    shared(par, q).wait_send()
                else:

                    @pl.when(k >= 2 if q < same else k < 2)
                    def _():
                        shared(par, q).wait_send()

            pl.semaphore_wait(credit.at[par], 1)

    def emit(phase, q, k, par, low, high):
        first = at.s == 0
        own[blocks_of(phase)[q], k] = jnp.where(first, low, high)
        stage[par, q] = jnp.where(first, high, low)

    def consume(phase, k, par, is_last):
        for q, i in enumerate(blocks_of(phase)):
            shared(par, q).wait_recv()

            def chunk(c, carry):
                here = pl.ds(pl.multiple_of(c * 96, 96), 96)
                total = own[i, k, here].astype(F32) + ring[par, q, here].astype(F32)
                own[i, k, here] = total.astype(own.dtype)
                return carry

            lax.fori_loop(0, own.shape[2] // 96, chunk, 0)
        if not is_last:
            pl.semaphore_signal(
                credit.at[par], inc=1, device_id=at.sibling(), device_id_type=MESH_ID
            )

    def column_sum(values):
        return jnp.sum(values, axis=0, keepdims=True)

    def ffn_step(sec, k, par, emits):
        middle = middle_buf
        gain, shift = vec[sec, 3:4], vec[sec, 4:5]

        @pl.when(k == 0)
        def _():
            source = cotangent if sec == n_section - 1 else grad_out.at[sec + 1]
            low = (source[...].astype(F32) * live[...]).astype(BF16)
            grad_low[...] = low
            left_t[...] = low.T
            unit, _ = unit_rows(middle[...])
            right_t[...] = (unit * gain + shift).astype(BF16).T
            acc[...] = jnp.zeros_like(acc)

        d_down = dot(left_t[...], hidden_buf[par, 0]).astype(BF16)
        emits(0, d_down[:, :half], d_down[:, half:])
        grad_hidden = (dot(grad_low[...], w_buf[par, 1]) * hidden_buf[par, 1].astype(F32)).astype(BF16)
        d_up_bias[sec, k] = column_sum(grad_hidden.astype(F32))
        d_up = dot(right_t[...], grad_hidden).astype(BF16)
        emits(1, d_up[:, :half], d_up[:, half:])
        acc[...] += dot_cols(grad_hidden, w_buf[par, 0])

    def attn_step(sec, k, par, emits):
        w_attn = w_buf.at[par, 0]

        @pl.when(k == 0)
        def _():
            unit, scale = unit_rows(middle_buf[...])
            grad_norm = acc[...]
            low = grad_low[...].astype(F32)
            mid = low + unit_rows_back(grad_norm * vec[sec, 3:4], unit, scale)
            grad_mid[...] = mid
            d_vec[sec, 2:3] = column_sum(mid)
            d_vec[sec, 3:4] = column_sum(grad_norm * unit)
            d_vec[sec, 4:5] = column_sum(grad_norm)
            d_vec[sec, 5:6] = column_sum(low)
            mid = mid.astype(BF16)
            grad_low[...] = mid
            left_t[...] = mid.T
            unit, _ = unit_rows(rows_buf[...].astype(F32))
            right_t[...] = (unit * vec[sec, 0:1] + vec[sec, 1:2]).astype(BF16).T
            acc[...] = jnp.zeros_like(acc)

        d_out = dot(left_t[...], heads_buf[par]).astype(BF16)
        grad_heads = dot(grad_low[...], w_attn[:, 3 * part :]).astype(BF16)
        per_image = []
        for image in range(images):
            span = slice(image * ROWS, (image + 1) * ROWS)
            per_head = [[], [], []]
            for head in range(n_heads):
                q, key, v = (
                    qkv_buf[par, span, c * part + head * DH : c * part + (head + 1) * DH]
                    for c in range(3)
                )
                grad_o = grad_heads[span, head * DH : (head + 1) * DH]
                chosen = p_buf[par, image, head]
                chances = chosen.astype(F32)
                grad_chances = dot_cols(v, grad_o)
                along = jnp.sum(chances * grad_chances, axis=0, keepdims=True)
                grad_scores = (chances * (grad_chances - along)).astype(BF16)
                per_head[0].append((dot(key.T, grad_scores).T * DH**-0.5).astype(BF16))
                per_head[1].append((dot(grad_scores, q) * DH**-0.5).astype(BF16))
                per_head[2].append(dot(chosen, grad_o).astype(BF16))
            per_image.append(jnp.concatenate(per_head[0] + per_head[1] + per_head[2], axis=1))
        grad_mixed = jnp.concatenate(per_image, axis=0)
        d_qkv_bias[sec, k] = column_sum(grad_mixed.astype(F32))
        d_qkv = dot(right_t[...], grad_mixed).astype(BF16)
        emits(0, d_qkv[:, :half], jnp.concatenate([d_qkv[:, half:], d_out], axis=1))
        acc[...] += dot_cols(grad_mixed, w_attn[:, : 3 * part])

        @pl.when(k == n_tensor - 1)
        def _():
            unit, scale = unit_rows(rows_buf[...].astype(F32))
            grad_norm = acc[...]
            d_vec[sec, 0:1] = column_sum(grad_norm * unit)
            d_vec[sec, 1:2] = column_sum(grad_norm)
            total = grad_mid[...] + unit_rows_back(grad_norm * vec[sec, 0:1], unit, scale)
            grad_out[sec] = total.astype(BF16)
            at.hand_out(grad_out, sec_grads, sec, row_sem)

    def compute(phase, k):
        kind, sec = phases[phase]
        par = lax.rem(k, 2)
        copies, once = loads(phase, k, par)
        for copy in copies:
            copy.wait()

        @pl.when(k == 0)
        def _():
            once().wait()

        @pl.when(k < n_tensor - 1)
        def _():
            start_loads(phase, k + 1, 1 - par, False)

        if phase + 1 < len(phases):

            @pl.when(k == n_tensor - 1)
            def _():
                start_loads(phase + 1, 0, 0, True)

        before_emit(phase, k, par)

        def emits(q, low, high):
            emit(phase, q, k, par, low, high)

        (ffn_step if kind == "ffn" else attn_step)(sec, k, par, emits)
        for q in range(len(blocks_of(phase))):
            shared(par, q).start()

        @pl.when(k > 0)
        def _():
            consume(phase, k - 1, 1 - par, False)

        if phase:

            @pl.when(k == 0)
            def _():
                consume(phase - 1, n_tensor - 1, 1 - par, False)

    def start_of(i):
        return BLOCK_TICKS * i + PAUSE * (i // n_blk)

    def block_at(tick):
        found, runs = 0, False
        for i in range(n_all):
            here = tick == start_of(i)
            found = jnp.where(here, i, found)
            runs = jnp.logical_or(runs, here)
        return found, runs

    small = [(d_vec, vec_in), (d_qkv_bias, qkv_bias_in), (d_up_bias, up_bias_in)]
    n_hops = len(at.bits)

    def small_copies(stage, device, slot):
        sec = 1 - at.s if stage == 0 else at.s
        return [
            pltpu.make_async_remote_copy(
                src_ref=mine.at[sec],
                dst_ref=came_in.at[slot],
                send_sem=small_sem.at[0, slot, n],
                recv_sem=small_sem.at[1, slot, n],
                device_id=device,
                device_id_type=MESH_ID,
            )
            for n, (mine, came_in) in enumerate(small)
        ]

    def small_send(stage):
        if stage == 0:
            return [small_copies(0, at.sibling(), 0)]
        if stage <= n_hops:
            return [small_copies(stage, at.hop(stage - 1), stage)]
        other = [lax.rem(at.t + k, n_tensor) for k in range(1, n_tensor)]
        return [
            small_copies(stage, (at.s, at.d, tt), n_hops + 1 + k) for k, tt in enumerate(other)
        ]

    def small_take(stage):
        sent = small_send(stage)
        for copies in sent:
            for copy in copies:
                copy.wait()
        first = stage if stage <= n_hops else n_hops + 1
        for mine, came_in in small:
            total = mine[at.s]
            for slot in range(first, first + len(sent)):
                total = total + came_in[slot]
            mine[at.s] = total

    def small_step(tick):
        for stage in range(n_hops + 2):

            @pl.when(tick == SMALL_TICKS * stage)
            def _():
                if stage:
                    small_take(stage - 1)
                for copies in small_send(stage):
                    for copy in copies:
                        copy.start()

        @pl.when(tick == SMALL_TICKS * (n_hops + 2))
        def _():
            small_take(n_hops + 1)

    def prologue(k, carry):
        compute(0, k)
        return carry

    start_loads(0, 0, 0, True)
    lax.fori_loop(0, n_tensor, prologue, 0)

    n_busy = (len(phases) - 1) * n_tensor

    def body(it, carry):
        for phase in range(1, len(phases)):

            @pl.when(lax.div(it, n_tensor) == phase - 1)
            def _():
                compute(phase, lax.rem(it, n_tensor))

        @pl.when(it == n_busy)
        def _():
            consume(len(phases) - 1, n_tensor - 1, (n_tensor - 1) % 2, True)

        for g, lag in sorted(enumerate(lags), key=lambda item: item[1]):
            i, runs = block_at(it - lag)

            @pl.when(runs)
            def _():
                run_group(i, g)

        small_step(it - n_busy)
        return carry

    lax.fori_loop(0, start_of(n_all - 1) + 1 + max(lags), body, 0)

    for par in range(2):
        for q in range(len(blocks_of(len(phases) - 1))):
            shared(par, q).wait_send()
    pl.semaphore_wait(credit.at[0], 1)

    def finish(i, carry):
        groups, _ = steps(i, False)
        for g in groups:
            g()
        sec, b = place(i)

        @pl.when(sec == at.s)
        def _():
            pltpu.make_async_copy(final.at[i], final.at[i], out_sem.at[2, i]).wait()

        return carry

    lax.fori_loop(0, n_all, finish, 0)
    at.handed_out(grad_out, sec_grads, row_sem)


def send_sizes(n_dp, n_tensor):
    bits = n_dp.bit_length() - 1
    mid = n_tensor // 2
    weights = [bin(e).count("1") for e in range(n_dp)]
    sizes = [2 * mid * sum(w >= 2 for w in weights), mid * bits]
    sizes += [mid * sum(w == k for w in weights) for k in range(bits, 0, -1)]
    return sizes + [2] * (n_tensor - 1) + [0]


def backward_and_reduce(weights, cotangent, live, vec, saved, n_dp):
    n_section, n_blk, n_tensor, width, span = weights.shape
    n_rows = cotangent.shape[0]
    images = n_rows // ROWS
    part = width // n_tensor
    n_all = n_section * n_blk
    depth, half = width // n_dp, span // 2
    slots = Slots(n_dp, n_tensor)
    n_sends = sum(send_sizes(n_dp, n_tensor))
    n_small = n_dp.bit_length() + n_tensor - 1
    shape = jax.ShapeDtypeStruct
    hbm = pl.BlockSpec(memory_space=pl.ANY)
    vmem = pl.BlockSpec(memory_space=pltpu.VMEM)
    dma = pltpu.SemaphoreType.DMA
    return pl.pallas_call(
        functools.partial(backward_kernel, n_dp, n_tensor, images),
        out_shape=[
            shape((n_blk, depth, span), F32),
            shape((n_section, n_rows, width), BF16),
            shape((n_section, 6, width), F32),
            shape((n_section, n_tensor, 1, 3 * part), F32),
            shape((n_section, n_tensor, 1, span), F32),
        ],
        in_specs=[hbm] + [vmem] * 3 + [hbm] * len(saved),
        out_specs=[hbm] * 2 + [vmem] * 3,
        scratch_shapes=[
            pltpu.VMEM((n_all, n_tensor, width, half), BF16),
            pltpu.VMEM((n_all, slots.count, depth, half), BF16),
            pltpu.VMEM((n_all, depth, half), F32),
            pltpu.VMEM((n_small, 6, width), F32),
            pltpu.VMEM((n_small, n_tensor, 1, 3 * part), F32),
            pltpu.VMEM((n_small, n_tensor, 1, span), F32),
            pltpu.VMEM((2, 2, width, half), BF16),
            pltpu.VMEM((2, 2, width, half), BF16),
            pltpu.VMEM((2, 2, width, span), BF16),
            pltpu.VMEM((2, 2, n_rows, span), BF16),
            pltpu.VMEM((2, n_rows, 3 * part), BF16),
            pltpu.VMEM((2, images, part // DH, ROWS, ROWS), BF16),
            pltpu.VMEM((2, n_rows, part), BF16),
            pltpu.VMEM((n_rows, width), BF16),
            pltpu.VMEM((n_rows, width), F32),
            pltpu.VMEM((n_section, n_rows, width), BF16),
            pltpu.VMEM((n_rows, width), BF16),
            pltpu.VMEM((width, n_rows), BF16),
            pltpu.VMEM((width, n_rows), BF16),
            pltpu.VMEM((n_rows, width), F32),
            pltpu.VMEM((n_rows, width), F32),
            dma((2, 5)),
            dma((2, 2, 2)),
            pltpu.SemaphoreType.REGULAR((2,)),
            dma((n_all, slots.count)),
            dma((n_all, n_sends)),
            dma((3, n_all)),
            dma((2, n_small, 3)),
            dma((3,)),
        ],
        compiler_params=pltpu.CompilerParams(
            collective_id=1, has_side_effects=True, vmem_limit_bytes=64 * 1024 * 1024 - 256 * 1024
        ),
    )(weights, cotangent, live, vec, *saved)


AXES = ("section", "tensor", "dp")


def shards(
    images,
    cotangent,
    counts,
    ln1_gain,
    ln1_bias,
    q_bias,
    v_bias,
    qkv_weight,
    out_weight,
    out_bias,
    ln2_gain,
    ln2_bias,
    up_weight,
    up_bias,
    down_weight,
    down_bias,
):
    n_section, n_dp, n_tensor = (lax.axis_size(a) for a in ("section", "dp", "tensor"))
    section_idx = lax.axis_index("section")
    micro_count, share_rows, width = images.shape
    own_count = micro_count // n_section
    depth = qkv_weight.shape[1]
    part = qkv_weight.shape[3]

    own = section_idx * own_count

    def own_rows(values):
        mine = lax.dynamic_slice_in_dim(values, own, own_count, 0).reshape(-1, SEQ, values.shape[-1])
        return jnp.pad(mine, ((0, 0), (0, ROWS - SEQ), (0, 0))).reshape(-1, values.shape[-1])

    row_place = lax.axis_index("tensor") * share_rows + jnp.arange(share_rows)
    own_counts = lax.dynamic_slice_in_dim(counts, own, own_count, 0)
    live_rows = (row_place // SEQ < own_counts).astype(jnp.float32)
    live_rows = live_rows.reshape(-1, SEQ)
    live_rows = jnp.pad(live_rows, ((0, 0), (0, ROWS - SEQ))).reshape(-1, 1)

    shard = jnp.stack(
        [
            jnp.concatenate([qkv_weight[0].reshape(depth, -1), out_weight[0].T], axis=1),
            up_weight[0],
            down_weight[0].T,
        ]
    )
    given = [ln1_gain, ln1_bias, out_bias, ln2_gain, ln2_bias, down_bias, q_bias, v_bias, up_bias]
    first_rows = own_rows(images)
    gathered, sec_rows, row_out, *kept, vec = gather_and_forward(
        shard, first_rows, live_rows, given, n_section, n_dp, n_tensor
    )
    weight_sum, sec_grads, d_vec, d_qkv_bias, d_up_bias = backward_and_reduce(
        gathered, own_rows(cotangent), live_rows, vec, [first_rows, row_out, *kept], n_dp
    )

    def placed_rows(values):
        values = values.reshape(-1, ROWS, width)[:, :SEQ]
        return values.reshape(1, micro_count, share_rows, width)

    section_out = placed_rows(sec_rows)
    input_grad = placed_rows(sec_grads)

    dp_idx, tensor_idx = lax.axis_index("dp"), lax.axis_index("tensor")

    def own_heads(sums, like):
        _, heads, lanes = like.shape
        sums = sums.reshape(-1, DH)
        return lax.dynamic_slice(sums, (0, dp_idx * lanes), (heads, lanes))[None]

    d_vec, d_qkv_bias, d_up_bias = (
        lax.dynamic_index_in_dim(v, section_idx, 0, keepdims=False)
        for v in (d_vec, d_qkv_bias, d_up_bias)
    )
    q_row, _, v_row = jnp.split(
        lax.dynamic_index_in_dim(d_qkv_bias, tensor_idx, 0, keepdims=False).reshape(-1), 3
    )
    up_row = lax.dynamic_index_in_dim(d_up_bias, tensor_idx, 0, keepdims=False)
    q_sum, v_sum, up_sum = own_heads(q_row, q_bias), own_heads(v_row, v_bias), own_heads(up_row, up_bias)
    block = width // (n_dp * n_tensor)
    vec = lax.dynamic_slice_in_dim(d_vec, (dp_idx * n_tensor + tensor_idx) * block, block, 1)[None]

    return (
        section_out,
        input_grad,
        weight_sum[0, :, : 3 * part].reshape(qkv_weight.shape),
        weight_sum[0, :, 3 * part :].T[None],
        weight_sum[1][None],
        weight_sum[2].T[None],
        q_sum,
        v_sum,
        up_sum,
        vec,
    )


def solution(mesh):
    placed = (
        P(None, ("dp", "tensor"), None),
        P(None, ("dp", "tensor"), None),
        P(None, "dp"),
        P("section", "dp"),
        P("section", "dp"),
        P("section", "tensor", "dp"),
        P("section", "tensor", "dp"),
        P("section", "dp", None, "tensor"),
        P("section", "tensor", "dp"),
        P("section", "dp"),
        P("section", "dp"),
        P("section", "dp"),
        P("section", "dp", "tensor"),
        P("section", "tensor", "dp"),
        P("section", "tensor", "dp"),
        P("section", "dp"),
    )
    return jax.shard_map(
        shards,
        mesh=mesh,
        in_specs=placed,
        out_specs=(
            P("section", None, ("dp", "tensor"), None),
            P("section", None, ("dp", "tensor"), None),
            P("section", "dp", None, "tensor"),
            P("section", "tensor", "dp"),
            P("section", "dp", "tensor"),
            P("section", "tensor", "dp"),
            P("section", "tensor", "dp"),
            P("section", "tensor", "dp"),
            P("section", "tensor", "dp"),
            P("section", None, ("dp", "tensor")),
        ),
        check_vma=False,
    )
```

profile of v0, /device:TPU:0, one launch (start us, length us, event | category | flops | bytes accessed | tf_op | source)
XLA Modules:
  0.0 324.9 jit_solution(8275808091676303463)
XLA Ops:
  0.6 0.0 copy-start
  0.7 0.0 copy-start.5
  0.7 1.0 copy.38
  1.7 1.1 copy.37
  2.8 0.2 copy.39
  3.0 0.0 copy-start.3
  3.0 0.0 copy-start.4
  3.1 0.1 maximum_bitcast_fusion
  3.2 0.0 copy-done.5
  3.2 2.1 pad_maximum_fusion.refs_0_
  5.3 0.0 copy-done.3
  5.3 0.0 copy-done.4
  5.3 1.2 constant_dynamic-slice_fusion.6
  6.5 0.1 copy.54
  6.6 0.9 pad.12.clone
  7.5 0.0 copy-done
  7.5 0.1 fusion.4
  7.6 0.1 broadcast_compare_fusion
  7.7 0.9 reshape.90.refs_2_.live
  8.6 149.2 %shard_map.231 = (bf16[2,3,4,768,768]{4,3,2,1,0:T(8,128)(2,1)}, bf16[2,416,768]{2,1,0:T(8,128)(2,1)}, bf16[2,416,768]{2,1,0:T(8,128)(2,1)}, bf16[2,4,416,576]{3,...) custom-call(bf16[3,192,768]{2,1,0:T(8,128)(2,1)} %pad_maximum_fusion, ...), custom_call_target="tpu_custom_call" | custom-call | tf_op jit(solution)/shard_map/pallas_call | solution.py:579
  157.8 1.4 slice.26
  159.2 1.5 copy.59
  160.7 0.1 copy.55
  160.7 0.9 pad.14.clone
  161.6 152.0 %shard_map.232 = (f32[3,192,768]{2,1,0:T(8,128)}, bf16[2,416,768]{2,1,0:T(8,128)(2,1)}, f32[2,6,768]{2,1,0:T(8,128)}, f32[2,4,1,576]{3,2,1,0:T(1,128)}, f32[2,4,1,768]{3,2,1,0:T(1,128)}) custom-call(bf16[2,3,4,768,768]{4,3,2,1,0:T(8,128)(2,1)} %get-tuple-element.26.weights, bf16[416,768]{1,0:T(8,128)(2,1)} %bitcast.42, f32[416,1]{1,0:T(8,128)} %reshape.90.refs_2_.live, ...), custom_call_target="tpu_custom_call" | custom-call | tf_op jit(solution)/shard_map/pallas_call | solution.py:1219
  313.7 1.4 slice.27
  315.0 0.0 copy-start.2
  315.0 1.5 copy.58
  316.5 0.1 copy-done.2
  316.6 0.2 copy.46
  316.9 1.1 copy.47
  317.9 0.1 slice_bitcast_fusion.1
  318.0 0.0 copy-start.1
  318.1 0.8 copy.48
  318.9 1.1 slice_bitcast_fusion
  319.9 0.7 fusion.2
  320.6 0.1 reshape.85
  320.7 0.1 fusion
  320.8 0.6 copy.49
  321.4 0.1 reshape.86
  321.4 0.1 fusion.1
  321.5 0.6 copy.50
  322.1 0.7 dynamic-slice_reduce_fusion
  322.8 0.1 reshape.87
  322.8 0.1 constant_dynamic-slice_fusion.2
  322.9 0.6 broadcast_in_dim.21
  323.5 0.8 constant_dynamic-slice_fusion.1
  324.3 0.6 copy.51
  324.9 0.0 copy-done.1
  (3 shorter events, 0.1 us)
Async XLA Ops:
  0.6 6.9 %copy-start = (s32[4,1]{0,1:T(1,128)S(1)}, s32[4,1]{0,1:T(1,128)}, u32[]{:S(2)}) copy-start(s32[4,1]{0,1:T(1,128)} %param.18) | copy-start | bytes 52
  0.7 2.5 copy-start.5
  3.0 2.3 copy-start.3
  3.0 2.2 copy-start.4
  315.0 1.6 copy-start.2
  318.0 6.8 %copy-start.1 = (s32[4,1]{0,1:T(1,128)S(1)}, s32[4,1]{0,1:T(1,128)}, u32[]{:S(2)}) copy-start(s32[4,1]{0,1:T(1,128)} %param.18) | copy-start | bytes 52
where the time goes:
time: 326 us; the launch traced here: 325 us
  Pallas kernels  301 us (92%)
  local copies, waits for them, and re-layouts  20.5 us (6%)
    pallas_call x1, Pallas kernels, backward_and_reduce(): pl.pallas_call(functools.partial(backward_kernel, n_dp, n_tensor, images)...  152 us
    pallas_call x1, Pallas kernels, gather_and_forward(): pl.pallas_call(functools.partial(forward_kernel, n_dp, n_tensor, images),...  149 us
    unnamed x23, local copies, waits for them, and re-layouts  8.96 us

commit v1 on v0

--- a/solution.py
+++ b/solution.py
@@ -7,11 +7,12 @@
 from jax.sharding import PartitionSpec as P
 
 CHUNK_ROWS = 48
-BLOCK_TICKS = 3
-PAUSE = 0
 SMALL_TICKS = 2
-GLAGS = [0, 2, 4, 5, 8, 9, 12, 14]
 MESH_ID = pl.DeviceIdType.MESH
+
+
+def sub_blocks(depth):
+    return 1
 
 
 def slot_sizes(n_dp, n_tensor):
@@ -149,16 +150,19 @@
 def forward_kernel(n_dp, n_tensor, images, *refs):
     (
         shard, rows, live, *given,
-        out, sec_rows, row_out, qkv_out, p_out, heads_out, middle_out, active_out, slope_out, vec,
+        out, row_out, qkv_out, p_out, heads_out, middle_out, active_out, slope_out, vec,
         w_buf, qkv_st, p_st, heads_st, active_st, slope_st, middle_st, normed, acc, row_buf,
         qkv_bias, up_bias, vec_in, qkv_bias_in, up_bias_in,
-        own_sem, recv_sem, send_sem, part_sem, load_sem, store_sem, active_sem, once_sem, row_sem, small_sem,
+        own_sem, recv_sem, send_sem, part_sem, load_sem, store_sem, active_sem, once_sem, small_sem,
     ) = refs
     at = Place(n_dp, n_tensor)
     n_section = out.shape[0]
     n_blk, depth, span = shard.shape
     half = span // 2
     n_all = n_section * n_blk
+    n_sub = sub_blocks(depth)
+    sub = depth // n_sub
+    n_pieces = n_all * n_sub
     part = vec.shape[2] // n_tensor
     n_heads = part // DH
 
@@ -188,7 +192,10 @@
     lanes = pl.ds(pl.multiple_of(at.s * half, 128), half)
 
     def piece(i, e, tt):
-        return out.at[lax.div(i, n_blk), lax.rem(i, n_blk), tt, rows_of(e), lanes]
+        block = lax.div(i, n_sub)
+        start = at.away(e) * depth + lax.rem(i, n_sub) * sub
+        rows_here = pl.ds(pl.multiple_of(start, 16), sub)
+        return out.at[lax.div(block, n_blk), lax.rem(block, n_blk), tt, rows_here, lanes]
 
     def share(b):
         return pltpu.make_async_remote_copy(
@@ -264,14 +271,16 @@
             maybe(cond, lambda: push_sib(i, e, tt, slot, start))
 
         def first():
-            sec, b = lax.div(i, n_blk), lax.rem(i, n_blk)
+            block = lax.div(i, n_sub)
+            sec, b = lax.div(block, n_blk), lax.rem(block, n_blk)
+            is_first = lax.rem(i, n_sub) == 0
             if start:
 
-                @pl.when(sec == at.s)
+                @pl.when(jnp.logical_and(sec == at.s, is_first))
                 def _():
                     pltpu.make_async_copy(shard.at[b], whole(at.s, b), own_sem.at[0, b]).wait()
 
-                @pl.when(sec != at.s)
+                @pl.when(jnp.logical_and(sec != at.s, is_first))
                 def _():
                     pltpu.make_async_remote_copy(
                         src_ref=shard.at[b],
@@ -387,6 +396,18 @@
                     for copies in small_send(stage):
                         for copy in copies:
                             copy.start()
+
+    lags = gather_lags(len(slot_sizes(n_dp, n_tensor)))
+    pace = n_tensor // n_sub
+    base = max(lags) + (n_sub - 1) * pace + 1
+    n_phases = n_all - 1
+    settle = max(lags) + n_tensor
+    n_ticks = base + n_phases * n_tensor
+
+    def finish(i):
+        groups, _ = steps(i, False)
+        for g in groups:
+            g()
 
     def load(i, k, par):
         return pltpu.make_async_copy(out.at[i // n_blk, i % n_blk, k], w_buf.at[par], load_sem.at[par])
@@ -471,21 +492,31 @@
         def _():
             row_buf[sec] = (acc[...] * live[...]).astype(BF16)
             store_rows(sec).start()
-            at.hand_out(row_buf, sec_rows, sec, row_sem)
+
+    def await_block(i):
+        sec, b = i // n_blk, i % n_blk
+        for each in range(i * n_sub, (i + 1) * n_sub):
+            for group, ref in (
+                (0, out.at[sec, b, pl.ds(0, n_tensor - 1), pl.ds(0, sub), pl.ds(0, half)]),
+                (1, out.at[sec, b, :, pl.ds(0, (n_dp - 1) * sub), pl.ds(0, half)]),
+            ):
+                pltpu.make_async_copy(ref, ref, part_sem.at[each, group]).wait()
 
     def compute(i, k):
         sec, b = i // n_blk, i % n_blk
         par = lax.rem(k, 2)
 
-        @pl.when(k == 0)
-        def _():
-            for group, ref in (
-                (0, out.at[sec, b, pl.ds(0, n_tensor - 1), pl.ds(0, depth), pl.ds(0, half)]),
-                (1, out.at[sec, b, :, pl.ds(0, (n_dp - 1) * depth), pl.ds(0, half)]),
-            ):
-                pltpu.make_async_copy(ref, ref, part_sem.at[i, group]).wait()
-            load(i, 0, 0).start()
-            if sec and b < 2:
+        if i == 0:
+
+            @pl.when(k == 0)
+            def _():
+                await_block(0)
+                load(0, 0, 0).start()
+
+        if sec and b < 2:
+
+            @pl.when(k == 0)
+            def _():
                 for back in (n_tensor - 2, n_tensor - 1):
                     for copy in stores(i - n_blk, back, back % 2):
                         copy.wait()
@@ -507,19 +538,29 @@
         for copy in stores(i, k, par):
             copy.start()
 
-    lags = gather_lags(len(slot_sizes(n_dp, n_tensor)))
-    base = max(lags) + 1
+        @pl.when(k == n_tensor - 1)
+        def _():
+            if i + 1 < n_all:
+                await_block(i + 1)
+            if i + 1 < n_phases:
+                load(i + 1, 0, 0).start()
 
     def body(it, carry):
         for g, lag in sorted(enumerate(lags), key=lambda item: item[1]):
-            i = lax.div(it - lag, n_tensor)
-
-            @pl.when(jnp.logical_and(it - lag == i * n_tensor, jnp.logical_and(it >= lag, i < n_all)))
+            i = lax.div(it - lag, pace)
+
+            @pl.when(jnp.logical_and(it - lag == i * pace, jnp.logical_and(it >= lag, i < n_pieces)))
             def _():
                 run_group(i, g)
 
         small_step(it)
-        for i in range(n_all):
+        i = lax.div(it - settle, pace)
+
+        @pl.when(jnp.logical_and(it - settle == i * pace, jnp.logical_and(it >= settle, i < n_pieces)))
+        def _():
+            finish(i)
+
+        for i in range(n_phases):
             first = base + i * n_tensor
 
             @pl.when(jnp.logical_and(it >= first, it < first + n_tensor))
@@ -534,15 +575,10 @@
             next(slots)
         groups[g]()
 
-    lax.fori_loop(0, base + n_all * n_tensor, body, 0)
-
-    def finish(i, carry):
-        groups, _ = steps(i, False)
-        for g in groups:
-            g()
-        return carry
-
-    lax.fori_loop(0, n_all, finish, 0)
+    lax.fori_loop(0, n_ticks, body, 0)
+    for i in range(n_pieces):
+        if settle + i * pace >= n_ticks:
+            finish(i)
     for b in range(n_blk):
         share(b).wait_send()
     last = n_section - 1
@@ -553,13 +589,13 @@
     for k in range(n_tensor):
         store_active(last, k).wait()
     store_middle(last).wait()
-    for sec in range(n_section):
+    for sec in range(last):
         store_rows(sec).wait()
-    at.handed_out(row_buf, sec_rows, row_sem)
 
 
 def gather_lags(n_groups):
-    return GLAGS
+    known = [0, 3, 6, 7, 10, 11, 14, 17]
+    return [known[g] if g < len(known) else known[-1] + 3 * (g - len(known) + 1) for g in range(n_groups)]
 
 
 def gather_and_forward(shard, rows, live, given, n_section, n_dp, n_tensor):
@@ -568,7 +604,7 @@
     images = n_rows // ROWS
     part = width // n_tensor
     n_heads = part // DH
-    n_all = n_section * n_blk
+    n_pieces = n_section * n_blk * sub_blocks(depth)
     n_hops = n_dp.bit_length() - 1
     n_sends = sum(slot_sizes(n_dp, n_tensor))
     n_small = n_hops + n_tensor
@@ -580,8 +616,7 @@
         functools.partial(forward_kernel, n_dp, n_tensor, images),
         out_shape=[
             shape((n_section, n_blk, n_tensor, width, span), BF16),
-            shape((n_section, n_rows, width), BF16),
-            shape((n_section, n_rows, width), BF16),
+            shape((n_section - 1, n_rows, width), BF16),
             shape((n_section, n_tensor, n_rows, 3 * part), BF16),
             shape((n_section, n_tensor, images, n_heads, ROWS, ROWS), BF16),
             shape((n_section, n_tensor, n_rows, part), BF16),
@@ -591,7 +626,7 @@
             shape((n_section, 6, width), F32),
         ],
         in_specs=[hbm] + [vmem] * (2 + len(given)),
-        out_specs=[hbm] * 9 + [vmem],
+        out_specs=[hbm] * 8 + [vmem],
         scratch_shapes=[
             pltpu.VMEM((2, width, span), BF16),
             pltpu.VMEM((2, n_rows, 3 * part), BF16),
@@ -602,21 +637,20 @@
             pltpu.VMEM((n_rows, width), F32),
             pltpu.VMEM((n_rows, width), BF16),
             pltpu.VMEM((n_rows, width), F32),
-            pltpu.VMEM((n_section, n_rows, width), BF16),
+            pltpu.VMEM((n_section - 1, n_rows, width), BF16),
             pltpu.VMEM((n_section, n_tensor, 1, 3 * part), F32),
             pltpu.VMEM((n_section, n_tensor, 1, span), F32),
             pltpu.VMEM((n_small, 6, width), F32),
             pltpu.VMEM((n_small, n_tensor, 1, 3 * part), F32),
             pltpu.VMEM((n_small, n_tensor, 1, span), F32),
             dma((3, n_blk)),
-            dma((n_all, n_dp * n_tensor)),
-            dma((n_all, n_sends)),
-            dma((n_all, 2)),
+            dma((n_pieces, n_dp * n_tensor)),
+            dma((n_pieces, n_sends)),
+            dma((n_pieces, 2)),
             dma((2,)),
             dma((2, 4)),
             dma((n_tensor,)),
             dma((1 + n_section,)),
-            dma((3,)),
             dma((2, n_small, 3)),
         ],
         compiler_params=pltpu.CompilerParams(
@@ -658,16 +692,19 @@
 ):
     first_rows, row_out, *saved = refs[:8]
     (
-        out, sec_grads, d_vec, d_qkv_bias, d_up_bias,
-        own, came, final, vec_in, qkv_bias_in, up_bias_in, ring, stage, w_buf, hidden_buf, qkv_buf, p_buf, heads_buf, rows_buf, middle_buf,
-        grad_out, grad_low, left_t, right_t, acc, grad_mid,
+        out, sec_rows, sec_grads, d_vec, d_qkv_bias, d_up_bias,
+        own, came, final, vec_in, qkv_bias_in, up_bias_in, ring, stage, w_buf, active_buf, slope_buf, qkv_buf, p_buf, heads_buf, rows_buf, middle_buf,
+        grad_out, last_rows, grad_low, left_t, right_t, acc, grad_mid,
         load_sem, stage_sem, credit, recv_sem, send_sem, out_sem, small_sem, row_sem,
     ) = refs[8:]
     at = Place(n_dp, n_tensor)
     slots = Slots(n_dp, n_tensor)
     n_section, n_blk = weights.shape[:2]
     n_all = n_section * n_blk
-    depth, half = final.shape[1:]
+    sub, half = final.shape[1:]
+    n_pieces = final.shape[0]
+    n_sub = n_pieces // n_all
+    depth = sub * n_sub
     part = vec.shape[2] // n_tensor
     n_heads = part // DH
     lanes = pl.ds(pl.multiple_of(at.s * half, 128), half)
@@ -675,16 +712,17 @@
     at.meet()
 
     def place(i):
-        return n_section - 1 - lax.div(i, n_blk), n_blk - 1 - lax.rem(i, n_blk)
+        block = lax.div(i, n_sub)
+        return n_section - 1 - lax.div(block, n_blk), n_blk - 1 - lax.rem(block, n_blk)
 
     def steps(i, start):
         counter = iter(range(10_000))
 
         def rows(e):
-            return pl.multiple_of(at.away(e) * depth, 16)
+            return pl.multiple_of(at.away(e) * depth + lax.rem(i, n_sub) * sub, 16)
 
         def piece(e, tt):
-            return own.at[i, tt, pl.ds(rows(e), depth), :]
+            return own.at[lax.div(i, n_sub), tt, pl.ds(rows(e), sub), :]
 
         def maybe(cond, action):
             if cond is None:
@@ -720,16 +758,16 @@
             def chunk(c, carry):
                 here = pl.ds(pl.multiple_of(base + c * CHUNK_ROWS, 16), CHUNK_ROWS)
                 local = pl.ds(pl.multiple_of(c * CHUNK_ROWS, 16), CHUNK_ROWS)
-                acc = own[i, tt, here, :].astype(jnp.float32)
+                acc = own[lax.div(i, n_sub), tt, here, :].astype(jnp.float32)
                 for slot in arrived:
                     acc = acc + came[i, slot, local, :].astype(jnp.float32)
                 if target is None:
-                    own[i, tt, here, :] = acc.astype(own.dtype)
+                    own[lax.div(i, n_sub), tt, here, :] = acc.astype(own.dtype)
                 else:
                     target[i, local, :] = acc
                 return carry
 
-            lax.fori_loop(0, depth // CHUNK_ROWS, chunk, 0)
+            lax.fori_loop(0, sub // CHUNK_ROWS, chunk, 0)
 
         def more(e, tt, slot, target=None):
             base = rows(e)
@@ -739,12 +777,12 @@
                 local = pl.ds(pl.multiple_of(c * CHUNK_ROWS, 16), CHUNK_ROWS)
                 acc = came[i, slot, local, :].astype(jnp.float32)
                 if target is None:
-                    own[i, tt, here, :] = (own[i, tt, here, :].astype(jnp.float32) + acc).astype(own.dtype)
+                    own[lax.div(i, n_sub), tt, here, :] = (own[lax.div(i, n_sub), tt, here, :].astype(jnp.float32) + acc).astype(own.dtype)
                 else:
                     target[i, local, :] = target[i, local, :] + acc
                 return carry
 
-            lax.fori_loop(0, depth // CHUNK_ROWS, chunk, 0)
+            lax.fori_loop(0, sub // CHUNK_ROWS, chunk, 0)
 
         def also(e, tt, slot, cond, target=None):
             if start:
@@ -823,10 +861,11 @@
             also(0, at.t, line_slot(at.t, True), at.has_next, final)
             also(0, at.t, line_slot(at.t, False), at.has_prev, final)
             sec, b = place(i)
-            stay = pltpu.make_async_copy(final.at[i], out.at[b, :, lanes], out_sem.at[0, i])
+            there = out.at[b, pl.ds(pl.multiple_of(lax.rem(i, n_sub) * sub, 16), sub), lanes]
+            stay = pltpu.make_async_copy(final.at[i], there, out_sem.at[0, i])
             go = pltpu.make_async_remote_copy(
                 src_ref=final.at[i],
-                dst_ref=out.at[b, :, lanes],
+                dst_ref=there,
                 send_sem=out_sem.at[1, i],
                 recv_sem=out_sem.at[2, i],
                 device_id=at.sibling(),
@@ -860,19 +899,25 @@
             next(counter)
         groups[g]()
 
-    phases = [(kind, sec) for sec in range(n_section - 1, -1, -1) for kind in ("ffn", "attn")]
+    phases = [(kind, sec) for sec in range(n_section - 1, -1, -1) for kind in ("down", "up", "attn")]
+    phases.append(("out", n_section - 1))
 
     def loads(phase, k, par):
         kind, sec = phases[phase]
         rows = first_rows if sec == 0 else row_out.at[sec - 1]
         qkv, p, heads, middle, active, slope = (ref.at[sec] for ref in saved)
-        if kind == "ffn":
+        if kind == "down":
+            pairs = [(active.at[k], active_buf.at[par])]
+            once = (middle, middle_buf)
+        elif kind == "up":
             pairs = [
                 (weights.at[sec, 1, k], w_buf.at[par, 0]),
                 (weights.at[sec, 2, k], w_buf.at[par, 1]),
-                (active.at[k], hidden_buf.at[par, 0]),
-                (slope.at[k], hidden_buf.at[par, 1]),
+                (slope.at[k], slope_buf.at[par]),
             ]
+            once = (rows, rows_buf)
+        elif kind == "out":
+            pairs = [(active.at[k], active_buf.at[par]), (weights.at[sec, 2, k], w_buf.at[par, 0])]
             once = (middle, middle_buf)
         else:
             pairs = [
@@ -881,7 +926,7 @@
                 (p.at[k], p_buf.at[par]),
                 (heads.at[k], heads_buf.at[par]),
             ]
-            once = (rows, rows_buf)
+            once = None
         copies = [
             pltpu.make_async_copy(src, dst, load_sem.at[par, n]) for n, (src, dst) in enumerate(pairs)
         ]
@@ -891,90 +936,83 @@
         copies, once = loads(phase, k, par)
         for copy in copies:
             copy.start()
-        if is_first:
+        if is_first and phases[phase][0] != "attn":
             once().start()
 
-    def blocks_of(phase):
-        kind, sec = phases[phase]
-        base = (n_section - 1 - sec) * n_blk
-        return [base, base + 1] if kind == "ffn" else [base + 2]
-
-    def shared(par, q):
+    def shared(k):
         return pltpu.make_async_remote_copy(
-            src_ref=stage.at[par, q],
-            dst_ref=ring.at[par, q],
-            send_sem=stage_sem.at[0, par, q],
-            recv_sem=stage_sem.at[1, par, q],
+            src_ref=stage.at[k],
+            dst_ref=ring.at[k],
+            send_sem=stage_sem.at[0, k],
+            recv_sem=stage_sem.at[1, k],
             device_id=at.sibling(),
             device_id_type=MESH_ID,
         )
 
-    def before_emit(phase, k, par):
-        if phase == 0:
-
-            @pl.when(k >= 2)
-            def _():
-                for q in range(2):
-                    shared(par, q).wait_send()
-                pl.semaphore_wait(credit.at[par], 1)
-
-        else:
-            same, back = len(blocks_of(phase)), len(blocks_of(phase - 1))
-            for q in range(max(same, back)):
-                if q < same and q < back:
-                    shared(par, q).wait_send()
-                else:
-
-                    @pl.when(k >= 2 if q < same else k < 2)
-                    def _():
-                        shared(par, q).wait_send()
-
-            pl.semaphore_wait(credit.at[par], 1)
-
-    def emit(phase, q, k, par, low, high):
+    def before_emit(k):
+        shared(k).wait_send()
+        pl.semaphore_wait(credit.at[k], 1)
+
+    def emit(phase, k, low, high):
         first = at.s == 0
-        own[blocks_of(phase)[q], k] = jnp.where(first, low, high)
-        stage[par, q] = jnp.where(first, high, low)
-
-    def consume(phase, k, par, is_last):
-        for q, i in enumerate(blocks_of(phase)):
-            shared(par, q).wait_recv()
-
-            def chunk(c, carry):
-                here = pl.ds(pl.multiple_of(c * 96, 96), 96)
-                total = own[i, k, here].astype(F32) + ring[par, q, here].astype(F32)
-                own[i, k, here] = total.astype(own.dtype)
-                return carry
-
-            lax.fori_loop(0, own.shape[2] // 96, chunk, 0)
+        own[phase, k] = jnp.where(first, low, high)
+        stage[k] = jnp.where(first, high, low)
+
+    def consume(phase, k, is_last):
+        shared(k).wait_recv()
+
+        def chunk(c, carry):
+            here = pl.ds(pl.multiple_of(c * 96, 96), 96)
+            total = own[phase, k, here].astype(F32) + ring[k, here].astype(F32)
+            own[phase, k, here] = total.astype(own.dtype)
+            return carry
+
+        lax.fori_loop(0, own.shape[2] // 96, chunk, 0)
         if not is_last:
             pl.semaphore_signal(
-                credit.at[par], inc=1, device_id=at.sibling(), device_id_type=MESH_ID
+                credit.at[k], inc=1, device_id=at.sibling(), device_id_type=MESH_ID
             )
 
     def column_sum(values):
         return jnp.sum(values, axis=0, keepdims=True)
 
-    def ffn_step(sec, k, par, emits):
-        middle = middle_buf
-        gain, shift = vec[sec, 3:4], vec[sec, 4:5]
-
+    def down_step(sec, k, par, emits):
         @pl.when(k == 0)
         def _():
             source = cotangent if sec == n_section - 1 else grad_out.at[sec + 1]
             low = (source[...].astype(F32) * live[...]).astype(BF16)
             grad_low[...] = low
             left_t[...] = low.T
-            unit, _ = unit_rows(middle[...])
-            right_t[...] = (unit * gain + shift).astype(BF16).T
+
+        d_down = dot(left_t[...], active_buf[par]).astype(BF16)
+        emits(d_down[:, :half], d_down[:, half:])
+
+    def out_step(sec, k, par):
+        @pl.when(k == 0)
+        def _():
+            acc[...] = middle_buf[...] + vec[sec, 5:6]
+
+        acc[...] += dot_cols(active_buf[par], w_buf[par, 0])
+
+        @pl.when(k == n_tensor - 1)
+        def _():
+            last_rows[sec] = (acc[...] * live[...]).astype(BF16)
+            for done in range(n_section - 1):
+                pltpu.make_async_copy(row_out.at[done], last_rows.at[done], row_sem.at[2, 0]).wait()
+            for each in range(n_section):
+                at.hand_out(last_rows, sec_rows, each, row_sem.at[1])
+
+    def up_step(sec, k, par, emits):
+        @pl.when(k == 0)
+        def _():
+            unit, _ = unit_rows(middle_buf[...])
+            right_t[...] = (unit * vec[sec, 3:4] + vec[sec, 4:5]).astype(BF16).T
             acc[...] = jnp.zeros_like(acc)
 
-        d_down = dot(left_t[...], hidden_buf[par, 0]).astype(BF16)
-        emits(0, d_down[:, :half], d_down[:, half:])
-        grad_hidden = (dot(grad_low[...], w_buf[par, 1]) * hidden_buf[par, 1].astype(F32)).astype(BF16)
+        grad_hidden = (dot(grad_low[...], w_buf[par, 1]) * slope_buf[par].astype(F32)).astype(BF16)
         d_up_bias[sec, k] = column_sum(grad_hidden.astype(F32))
         d_up = dot(right_t[...], grad_hidden).astype(BF16)
-        emits(1, d_up[:, :half], d_up[:, half:])
+        emits(d_up[:, :half], d_up[:, half:])
         acc[...] += dot_cols(grad_hidden, w_buf[par, 0])
 
     def attn_step(sec, k, par, emits):
@@ -1022,7 +1060,7 @@
         grad_mixed = jnp.concatenate(per_image, axis=0)
         d_qkv_bias[sec, k] = column_sum(grad_mixed.astype(F32))
         d_qkv = dot(right_t[...], grad_mixed).astype(BF16)
-        emits(0, d_qkv[:, :half], jnp.concatenate([d_qkv[:, half:], d_out], axis=1))
+        emits(d_qkv[:, :half], jnp.concatenate([d_qkv[:, half:], d_out], axis=1))
         acc[...] += dot_cols(grad_mixed, w_attn[:, : 3 * part])
 
         @pl.when(k == n_tensor - 1)
@@ -1033,7 +1071,7 @@
             d_vec[sec, 1:2] = column_sum(grad_norm)
             total = grad_mid[...] + unit_rows_back(grad_norm * vec[sec, 0:1], unit, scale)
             grad_out[sec] = total.astype(BF16)
-            at.hand_out(grad_out, sec_grads, sec, row_sem)
+            at.hand_out(grad_out, sec_grads, sec, row_sem.at[0])
 
     def compute(phase, k):
         kind, sec = phases[phase]
@@ -1042,9 +1080,11 @@
         for copy in copies:
             copy.wait()
 
-        @pl.when(k == 0)
-        def _():
-            once().wait()
+        if kind != "attn":
+
+            @pl.when(k == 0)
+            def _():
+                once().wait()
 
         @pl.when(k < n_tensor - 1)
         def _():
@@ -1056,35 +1096,72 @@
             def _():
                 start_loads(phase + 1, 0, 0, True)
 
-        before_emit(phase, k, par)
-
-        def emits(q, low, high):
-            emit(phase, q, k, par, low, high)
-
-        (ffn_step if kind == "ffn" else attn_step)(sec, k, par, emits)
-        for q in range(len(blocks_of(phase))):
-            shared(par, q).start()
-
-        @pl.when(k > 0)
-        def _():
-            consume(phase, k - 1, 1 - par, False)
+        if kind == "out":
+            out_step(sec, k, par)
+
+            @pl.when(k == 0)
+            def _():
+                for back in (n_tensor - 2, n_tensor - 1):
+                    consume(phase - 1, back, True)
+
+            return
 
         if phase:
+            before_emit(k)
+
+        if phase == 0:
 
             @pl.when(k == 0)
             def _():
-                consume(phase - 1, n_tensor - 1, 1 - par, False)
+                for done in range(n_section - 1):
+                    pltpu.make_async_copy(
+                        row_out.at[done], last_rows.at[done], row_sem.at[2, 0]
+                    ).start()
+
+        def emits(low, high):
+            emit(phase, k, low, high)
+
+        {"down": down_step, "up": up_step, "attn": attn_step}[kind](sec, k, par, emits)
+        shared(k).start()
+
+        @pl.when(k >= 2)
+        def _():
+            consume(phase, k - 2, phase == n_all - 1)
+
+        if phase:
+
+            @pl.when(k == 0)
+            def _():
+                for back in (n_tensor - 2, n_tensor - 1):
+                    consume(phase - 1, back, False)
+
+    n_busy = n_all * n_tensor
+    settle = max(lags) + 2
+    short = n_tensor // 2
+    per_section = short + 2 * n_tensor
+
+    def tick_of(it):
+        sec, step = lax.div(it, n_blk * n_tensor), lax.rem(it, n_blk * n_tensor)
+        is_short = step < n_tensor
+        tick = sec * per_section + jnp.where(is_short, lax.div(step, 2), step - n_tensor + short)
+        over = it >= len(phases) * n_tensor
+        tick = jnp.where(over, n_section * per_section + short + it - len(phases) * n_tensor, tick)
+        return tick, jnp.logical_or(over, jnp.logical_or(jnp.logical_not(is_short), lax.rem(step, 2) == 1))
 
     def start_of(i):
-        return BLOCK_TICKS * i + PAUSE * (i // n_blk)
-
-    def block_at(tick):
-        found, runs = 0, False
-        for i in range(n_all):
+        block, within = i // n_sub, i % n_sub
+        sec, b = block // n_blk, block % n_blk
+        first = sec * per_section + (short, short + n_tensor, per_section)[b]
+        return first + within * (2 if b == 0 else 2 if b == 1 else 1)
+
+    def piece_at(tick):
+        found, starts = 0, False
+        for i in range(n_pieces):
             here = tick == start_of(i)
             found = jnp.where(here, i, found)
-            runs = jnp.logical_or(runs, here)
-        return found, runs
+            starts = jnp.logical_or(starts, here)
+        return found, starts
+
 
     small = [(d_vec, vec_in), (d_qkv_bias, qkv_bias_in), (d_up_bias, up_bias_in)]
     n_hops = len(at.bits)
@@ -1140,44 +1217,7 @@
         def _():
             small_take(n_hops + 1)
 
-    def prologue(k, carry):
-        compute(0, k)
-        return carry
-
-    start_loads(0, 0, 0, True)
-    lax.fori_loop(0, n_tensor, prologue, 0)
-
-    n_busy = (len(phases) - 1) * n_tensor
-
-    def body(it, carry):
-        for phase in range(1, len(phases)):
-
-            @pl.when(lax.div(it, n_tensor) == phase - 1)
-            def _():
-                compute(phase, lax.rem(it, n_tensor))
-
-        @pl.when(it == n_busy)
-        def _():
-            consume(len(phases) - 1, n_tensor - 1, (n_tensor - 1) % 2, True)
-
-        for g, lag in sorted(enumerate(lags), key=lambda item: item[1]):
-            i, runs = block_at(it - lag)
-
-            @pl.when(runs)
-            def _():
-                run_group(i, g)
-
-        small_step(it - n_busy)
-        return carry
-
-    lax.fori_loop(0, start_of(n_all - 1) + 1 + max(lags), body, 0)
-
-    for par in range(2):
-        for q in range(len(blocks_of(len(phases) - 1))):
-            shared(par, q).wait_send()
-    pl.semaphore_wait(credit.at[0], 1)
-
-    def finish(i, carry):
+    def finish(i):
         groups, _ = steps(i, False)
         for g in groups:
             g()
@@ -1187,10 +1227,43 @@
         def _():
             pltpu.make_async_copy(final.at[i], final.at[i], out_sem.at[2, i]).wait()
 
+    def body(it, carry):
+        for phase in range(len(phases)):
+
+            @pl.when(lax.div(it, n_tensor) == phase)
+            def _():
+                compute(phase, lax.rem(it, n_tensor))
+
+        tick, ticks = tick_of(it)
+        for g, lag in sorted(enumerate(lags), key=lambda item: item[1]):
+            i, starts = piece_at(tick - lag)
+
+            @pl.when(jnp.logical_and(ticks, starts))
+            def _():
+                run_group(i, g)
+
+        small_step(it - n_busy)
+        i, starts = piece_at(tick - settle)
+
+        @pl.when(jnp.logical_and(ticks, starts))
+        def _():
+            finish(i)
+
         return carry
 
-    lax.fori_loop(0, n_all, finish, 0)
-    at.handed_out(grad_out, sec_grads, row_sem)
+    start_loads(0, 0, 0, True)
+    last_tick = start_of(n_pieces - 1) + max(lags)
+    tail = max(last_tick + 1, n_section * per_section + short + SMALL_TICKS * (n_hops + 2)) - n_section * per_section - short
+    n_ticks = len(phases) * n_tensor + tail
+    last_tick = n_section * per_section + short + tail - 1
+    lax.fori_loop(0, n_ticks, body, 0)
+    for i in range(n_pieces):
+        if start_of(i) + settle > last_tick:
+            finish(i)
+    for k in range(n_tensor):
+        shared(k).wait_send()
+    at.handed_out(grad_out, sec_grads, row_sem.at[0])
+    at.handed_out(last_rows, sec_rows, row_sem.at[1])
 
 
 def send_sizes(n_dp, n_tensor):
@@ -1209,6 +1282,8 @@
     part = width // n_tensor
     n_all = n_section * n_blk
     depth, half = width // n_dp, span // 2
+    n_pieces = n_all * sub_blocks(depth)
+    sub = depth // sub_blocks(depth)
     slots = Slots(n_dp, n_tensor)
     n_sends = sum(send_sizes(n_dp, n_tensor))
     n_small = n_dp.bit_length() + n_tensor - 1
@@ -1221,28 +1296,31 @@
         out_shape=[
             shape((n_blk, depth, span), F32),
             shape((n_section, n_rows, width), BF16),
+            shape((n_section, n_rows, width), BF16),
             shape((n_section, 6, width), F32),
             shape((n_section, n_tensor, 1, 3 * part), F32),
             shape((n_section, n_tensor, 1, span), F32),
         ],
         in_specs=[hbm] + [vmem] * 3 + [hbm] * len(saved),
-        out_specs=[hbm] * 2 + [vmem] * 3,
+        out_specs=[hbm] * 3 + [vmem] * 3,
         scratch_shapes=[
             pltpu.VMEM((n_all, n_tensor, width, half), BF16),
-            pltpu.VMEM((n_all, slots.count, depth, half), BF16),
-            pltpu.VMEM((n_all, depth, half), F32),
+            pltpu.VMEM((n_pieces, slots.count, sub, half), BF16),
+            pltpu.VMEM((n_pieces, sub, half), F32),
             pltpu.VMEM((n_small, 6, width), F32),
             pltpu.VMEM((n_small, n_tensor, 1, 3 * part), F32),
             pltpu.VMEM((n_small, n_tensor, 1, span), F32),
-            pltpu.VMEM((2, 2, width, half), BF16),
-            pltpu.VMEM((2, 2, width, half), BF16),
+            pltpu.VMEM((n_tensor, width, half), BF16),
+            pltpu.VMEM((n_tensor, width, half), BF16),
             pltpu.VMEM((2, 2, width, span), BF16),
-            pltpu.VMEM((2, 2, n_rows, span), BF16),
+            pltpu.VMEM((2, n_rows, span), BF16),
+            pltpu.VMEM((2, n_rows, span), BF16),
             pltpu.VMEM((2, n_rows, 3 * part), BF16),
             pltpu.VMEM((2, images, part // DH, ROWS, ROWS), BF16),
             pltpu.VMEM((2, n_rows, part), BF16),
             pltpu.VMEM((n_rows, width), BF16),
             pltpu.VMEM((n_rows, width), F32),
+            pltpu.VMEM((n_section, n_rows, width), BF16),
             pltpu.VMEM((n_section, n_rows, width), BF16),
             pltpu.VMEM((n_rows, width), BF16),
             pltpu.VMEM((width, n_rows), BF16),
@@ -1250,13 +1328,13 @@
             pltpu.VMEM((n_rows, width), F32),
             pltpu.VMEM((n_rows, width), F32),
             dma((2, 5)),
-            dma((2, 2, 2)),
-            pltpu.SemaphoreType.REGULAR((2,)),
-            dma((n_all, slots.count)),
-            dma((n_all, n_sends)),
-            dma((3, n_all)),
+            dma((2, n_tensor)),
+            pltpu.SemaphoreType.REGULAR((n_tensor,)),
+            dma((n_pieces, slots.count)),
+            dma((n_pieces, n_sends)),
+            dma((3, n_pieces)),
             dma((2, n_small, 3)),
-            dma((3,)),
+            dma((3, 3)),
         ],
         compiler_params=pltpu.CompilerParams(
             collective_id=1, has_side_effects=True, vmem_limit_bytes=64 * 1024 * 1024 - 256 * 1024
@@ -1313,10 +1391,10 @@
     )
     given = [ln1_gain, ln1_bias, out_bias, ln2_gain, ln2_bias, down_bias, q_bias, v_bias, up_bias]
     first_rows = own_rows(images)
-    gathered, sec_rows, row_out, *kept, vec = gather_and_forward(
+    gathered, row_out, *kept, vec = gather_and_forward(
         shard, first_rows, live_rows, given, n_section, n_dp, n_tensor
     )
-    weight_sum, sec_grads, d_vec, d_qkv_bias, d_up_bias = backward_and_reduce(
+    weight_sum, sec_rows, sec_grads, d_vec, d_qkv_bias, d_up_bias = backward_and_reduce(
         gathered, own_rows(cotangent), live_rows, vec, [first_rows, row_out, *kept], n_dp
     )
 

time: 326 us -> 321 us (0.985); the launches traced: 325 us -> 324 us
    pallas_call x1, Pallas kernels: 152 us -> 162 us  [backward_and_reduce(): pl.pallas_call(functools.partial(backward_kernel, n_dp, n_tensor, images)...]
    pallas_call x1, Pallas kernels: 149 us -> 140 us  [gather_and_forward(): pl.pallas_call(functools.partial(forward_kernel, n_dp, n_tensor, images),...]
    unnamed x23 -> x27, local copies, waits for them, and re-layouts: 8.96 us -> 7.72 us
where the time goes in v1:
time: 321 us; the launch traced here: 324 us
  Pallas kernels  302 us (94%)
  local copies, waits for them, and re-layouts  19.6 us (6%)
    pallas_call x1, Pallas kernels, backward_and_reduce(): pl.pallas_call(functools.partial(backward_kernel, n_dp, n_tensor, images)...  162 us
    pallas_call x1, Pallas kernels, gather_and_forward(): pl.pallas_call(functools.partial(forward_kernel, n_dp, n_tensor, images),...  140 us
    unnamed x27, local copies, waits for them, and re-layouts  7.72 us

profile of v1, /device:TPU:0, one launch (start us, length us, event | category | flops | bytes accessed | tf_op | source)
XLA Modules:
  0.0 323.8 jit_solution(14926662211756677454)
XLA Ops:
  0.6 0.0 copy-start
  0.7 0.6 copy-done
  1.3 0.1 fusion.4
  1.4 0.1 broadcast_compare_fusion
  1.5 0.9 reshape.90.refs_2_.live
  2.4 2.9 constant_dynamic-slice_fusion.6
  5.3 0.0 copy-start.6
  5.3 0.0 copy-start.7
  5.3 0.1 copy.54
  5.4 0.0 copy-start.4
  5.4 0.0 copy-start.5
  5.4 0.9 pad.12.clone
  6.3 0.0 copy-done.6
  6.3 0.2 copy.37
  6.4 0.2 copy.39
  6.6 0.0 copy-done.7
  6.6 0.1 copy.38
  6.7 0.1 maximum_bitcast_fusion
  6.8 0.0 copy-done.4
  6.8 0.0 copy-done.5
  6.9 1.0 pad_maximum_fusion.refs_0_
  7.9 140.4 %shard_map.231 = (bf16[2,3,4,768,768]{4,3,2,1,0:T(8,128)(2,1)}, bf16[1,416,768]{2,1,0:T(8,128)(2,1)}, bf16[2,4,416,576]{3,2,1,0:T(8,128)(2,1)}, bf16[2,4,2,3,208...) custom-call(bf16[3,192,768]{2,1,0:T(8,128)(2,1)} %pad_maximum_fusion, ...), custom_call_target="tpu_custom_call" | custom-call | tf_op jit(solution)/shard_map/pallas_call | solution.py:615
  148.2 0.1 copy.55
  148.3 0.9 pad.14.clone
  149.2 161.6 %shard_map.232 = (f32[3,192,768]{2,1,0:T(8,128)}, bf16[2,416,768]{2,1,0:T(8,128)(2,1)}, bf16[2,416,768]{2,1,0:T(8,128)(2,1)}, f32[2,6,768]{2,1,0:T(8,128)}, f32[...) custom-call(bf16[2,3,4,768,768]{4,3,2,1,0:T(8,128)(2,1)} %get-tuple-element.25.weights, bf16[416,768]{1,0:T(8,128)(2,1)} %bitcast.42, ...), custom_call_target="tpu_custom_call" | custom-call | tf_op jit(solution)/shard_map/pallas_call | solution.py:1294
  310.8 1.4 slice.27
  312.1 0.0 copy-start.3
  312.1 1.5 copy.58
  313.6 0.0 copy-done.3
  313.6 0.1 slice.26
  313.7 0.0 copy-start.2
  313.7 1.5 copy.59
  315.2 0.1 copy-done.2
  315.3 0.2 copy.46
  315.6 0.0 copy-start.1
  315.6 1.1 copy.47
  316.6 1.1 slice_bitcast_fusion
  317.7 0.1 slice_bitcast_fusion.1
  317.8 0.8 copy.48
  318.6 0.7 dynamic-slice_reduce_fusion
  319.3 0.1 reshape.87
  319.4 0.1 constant_dynamic-slice_fusion.2
  319.5 0.6 broadcast_in_dim.21
  320.1 0.8 constant_dynamic-slice_fusion.1
  320.8 0.6 copy.51
  321.4 0.7 fusion.2
  322.1 0.1 reshape.85
  322.2 0.1 fusion
  322.3 0.6 copy.49
  322.8 0.1 reshape.86
  322.9 0.1 fusion.1
  323.0 0.6 copy.50
  323.6 0.0 copy-done.1
  (3 shorter events, 0.1 us)
Async XLA Ops:
  0.6 0.7 copy-start
  5.3 1.0 copy-start.6
  5.3 1.3 copy-start.7
  5.4 1.5 copy-start.4
  5.4 1.5 copy-start.5
  312.1 1.5 copy-start.3
  313.7 1.6 copy-start.2
  315.6 8.0 %copy-start.1 = (s32[4,1]{0,1:T(1,128)S(1)}, s32[4,1]{0,1:T(1,128)}, u32[]{:S(2)}) copy-start(s32[4,1]{0,1:T(1,128)} %param.18) | copy-start | bytes 52

commit v2 on v1

--- a/solution.py
+++ b/solution.py
@@ -35,7 +35,8 @@
     first = [2 + len(bits)]
     columns = [2 * (2 + len(bits))] * (n_tensor - 1)
     planes = [plane(w) for w in range(1, len(bits) + 1)]
-    crossed = [3 * mid * sum(w >= 2 for w in weights)]
+    over = mid * sum(w >= 2 for w in weights)
+    crossed = [3 * over] * (mid - 1) + [over]
     rest = [mid * sum(w == 1 for w in weights)]
     return first + [columns[0], planes[0], columns[1]] + planes[1:] + columns[2:] + crossed + rest
 
@@ -321,17 +322,18 @@
                         go(e, tt, at.along(-1), e, at.t == at.mid)
                     go_sib(e, tt)
 
-        def crossed():
+        def crossed(k):
+            down, up = at.t == at.mid - 1 - k, at.t == at.mid + k
+            here = jnp.logical_or(down, up)
             for weight in range(2, len(at.bits) + 1):
                 for e in at.by_weight(weight):
                     for j in range(at.mid):
                         tt = at.other_side(j)
-                        ready(e, tt)
-                        up = jnp.logical_and(at.t >= at.mid, at.has_next)
-                        down = jnp.logical_and(at.t < at.mid, at.has_prev)
-                        go(e, tt, at.along(1), e, up)
-                        go(e, tt, at.along(-1), e, down)
-                        go_sib(e, tt)
+                        ready(e, tt, here)
+                        if k < at.mid - 1:
+                            go(e, tt, at.along(1), e, up)
+                            go(e, tt, at.along(-1), e, down)
+                        go_sib(e, tt, here)
 
         def rest():
             for e in at.by_weight(1):
@@ -345,7 +347,8 @@
             groups.append(functools.partial(column, k))
         planes = [functools.partial(plane, w) for w in range(1, len(at.bits) + 1)]
         merged = [groups[0]]
-        order = [groups[1], planes[0], groups[2]] + planes[1:] + groups[3:] + [crossed, rest]
+        far = [functools.partial(crossed, k) for k in range(at.mid)]
+        order = [groups[1], planes[0], groups[2]] + planes[1:] + groups[3:] + far + [rest]
         return merged + order, slots
 
 
@@ -594,7 +597,7 @@
 
 
 def gather_lags(n_groups):
-    known = [0, 3, 6, 7, 10, 11, 14, 17]
+    known = [0, 3, 6, 7, 10, 11, 13, 16, 17]
     return [known[g] if g < len(known) else known[-1] + 3 * (g - len(known) + 1) for g in range(n_groups)]
 
 
@@ -684,7 +687,8 @@
 
 
 def reduce_lags(n_groups):
-    return [0, 0] + [2 + 3 * min(g, 2) + 2 * max(g - 2, 0) for g in range(n_groups - 2)]
+    known = [0, 0, 2, 5, 5, 6, 12, 19]
+    return [known[g] if g < len(known) else known[-1] + 3 * (g - len(known) + 1) for g in range(n_groups)]
 
 
 def backward_kernel(
@@ -1152,7 +1156,7 @@
         block, within = i // n_sub, i % n_sub
         sec, b = block // n_blk, block % n_blk
         first = sec * per_section + (short, short + n_tensor, per_section)[b]
-        return first + within * (2 if b == 0 else 2 if b == 1 else 1)
+        return first + (2 if i == 1 else 0) + within
 
     def piece_at(tick):
         found, starts = 0, False

time: 321 us -> 307 us (0.956)
  Pallas kernels: 302 us -> 288 us
    pallas_call x1, Pallas kernels: 162 us -> 151 us  [backward_and_reduce(): pl.pallas_call(functools.partial(backward_kernel, n_dp, n_tensor, images)...]
    pallas_call x1, Pallas kernels: 140 us -> 137 us  [gather_and_forward(): pl.pallas_call(functools.partial(forward_kernel, n_dp, n_tensor, images),...]
where the time goes in v2:
time: 307 us; the launch traced here: 310 us
  Pallas kernels  288 us (94%)
  local copies, waits for them, and re-layouts  19.6 us (6%)
    pallas_call x1, Pallas kernels, backward_and_reduce(): pl.pallas_call(functools.partial(backward_kernel, n_dp, n_tensor, images)...  151 us
    pallas_call x1, Pallas kernels, gather_and_forward(): pl.pallas_call(functools.partial(forward_kernel, n_dp, n_tensor, images),...  137 us
    unnamed x27, local copies, waits for them, and re-layouts  7.72 us

profile of v2, /device:TPU:0, one launch (start us, length us, event | category | flops | bytes accessed | tf_op | source)
XLA Modules:
  0.0 309.8 jit_solution(9206985823224862350)
XLA Ops:
  0.6 0.0 copy-start
  0.7 0.6 copy-done
  1.3 0.1 fusion.4
  1.4 0.1 broadcast_compare_fusion
  1.5 0.9 reshape.90.refs_2_.live
  2.4 2.9 constant_dynamic-slice_fusion.6
  5.3 0.0 copy-start.6
  5.3 0.0 copy-start.7
  5.3 0.1 copy.54
  5.4 0.0 copy-start.4
  5.4 0.0 copy-start.5
  5.4 0.9 pad.12.clone
  6.3 0.0 copy-done.6
  6.3 0.2 copy.37
  6.4 0.2 copy.39
  6.6 0.0 copy-done.7
  6.6 0.1 copy.38
  6.7 0.1 maximum_bitcast_fusion
  6.8 0.0 copy-done.4
  6.8 0.0 copy-done.5
  6.9 1.0 pad_maximum_fusion.refs_0_
  7.9 137.2 %shard_map.231 = (bf16[2,3,4,768,768]{4,3,2,1,0:T(8,128)(2,1)}, bf16[1,416,768]{2,1,0:T(8,128)(2,1)}, bf16[2,4,416,576]{3,2,1,0:T(8,128)(2,1)}, bf16[2,4,2,3,208...) custom-call(bf16[3,192,768]{2,1,0:T(8,128)(2,1)} %pad_maximum_fusion, ...), custom_call_target="tpu_custom_call" | custom-call | tf_op jit(solution)/shard_map/pallas_call | solution.py:618
  145.0 0.1 copy.55
  145.1 0.9 pad.14.clone
  146.0 150.8 %shard_map.232 = (f32[3,192,768]{2,1,0:T(8,128)}, bf16[2,416,768]{2,1,0:T(8,128)(2,1)}, bf16[2,416,768]{2,1,0:T(8,128)(2,1)}, f32[2,6,768]{2,1,0:T(8,128)}, f32[...) custom-call(bf16[2,3,4,768,768]{4,3,2,1,0:T(8,128)(2,1)} %get-tuple-element.25.weights, bf16[416,768]{1,0:T(8,128)(2,1)} %bitcast.42, ...), custom_call_target="tpu_custom_call" | custom-call | tf_op jit(solution)/shard_map/pallas_call | solution.py:1298
  296.7 1.4 slice.27
  298.1 0.0 copy-start.3
  298.1 1.5 copy.58
  299.6 0.0 copy-done.3
  299.6 0.1 slice.26
  299.7 0.0 copy-start.2
  299.7 1.5 copy.59
  301.2 0.1 copy-done.2
  301.3 0.2 copy.46
  301.5 0.0 copy-start.1
  301.5 1.1 copy.47
  302.6 1.1 slice_bitcast_fusion
  303.7 0.1 slice_bitcast_fusion.1
  303.8 0.8 copy.48
  304.6 0.7 dynamic-slice_reduce_fusion
  305.3 0.1 reshape.87
  305.4 0.1 constant_dynamic-slice_fusion.2
  305.4 0.6 broadcast_in_dim.21
  306.0 0.8 constant_dynamic-slice_fusion.1
  306.8 0.6 copy.51
  307.4 0.7 fusion.2
  308.1 0.1 reshape.85
  308.2 0.1 fusion
  308.2 0.6 copy.49
  308.8 0.1 reshape.86
  308.9 0.1 fusion.1
  309.0 0.6 copy.50
  309.5 0.0 copy-done.1
  (3 shorter events, 0.1 us)
Async XLA Ops:
  0.6 0.7 copy-start
  5.3 1.0 copy-start.6
  5.3 1.3 copy-start.7
  5.4 1.5 copy-start.4
  5.4 1.5 copy-start.5
  298.1 1.5 copy-start.3
  299.7 1.6 copy-start.2
  301.5 8.0 %copy-start.1 = (s32[4,1]{0,1:T(1,128)S(1)}, s32[4,1]{0,1:T(1,128)}, u32[]{:S(2)}) copy-start(s32[4,1]{0,1:T(1,128)} %param.18) | copy-start | bytes 52

commit v3 on v2

--- a/solution.py
+++ b/solution.py
@@ -696,7 +696,7 @@
 ):
     first_rows, row_out, *saved = refs[:8]
     (
-        out, sec_rows, sec_grads, d_vec, d_qkv_bias, d_up_bias,
+        out, sec_rows, sec_grads, d_vec, d_qkv_bias, d_up_bias, own_vec, own_q, own_v, own_up,
         own, came, final, vec_in, qkv_bias_in, up_bias_in, ring, stage, w_buf, active_buf, slope_buf, qkv_buf, p_buf, heads_buf, rows_buf, middle_buf,
         grad_out, last_rows, grad_low, left_t, right_t, acc, grad_mid,
         load_sem, stage_sem, credit, recv_sem, send_sem, out_sem, small_sem, row_sem,
@@ -1220,6 +1220,24 @@
         @pl.when(tick == SMALL_TICKS * (n_hops + 2))
         def _():
             small_take(n_hops + 1)
+            own_small()
+
+    def own_small():
+        def pick(values, index, count, width):
+            parts = [jnp.where(index == c, values[:, c * width : (c + 1) * width], 0.0) for c in range(count)]
+            return functools.reduce(jnp.add, parts)
+
+        n_places = n_dp * n_tensor
+        own_vec[0] = pick(d_vec[at.s], at.d * n_tensor + at.t, n_places, own_vec.shape[2])
+        qkv_row, up_row = d_qkv_bias[at.s, at.t], d_up_bias[at.s, at.t]
+        for target, row in (
+            (own_q, qkv_row[:, :part]),
+            (own_v, qkv_row[:, 2 * part :]),
+            (own_up, up_row),
+        ):
+            for head in range(target.shape[1]):
+                lanes_of = row[:, head * DH : (head + 1) * DH]
+                target[0, head : head + 1] = pick(lanes_of, at.d, n_dp, DH // n_dp)
 
     def finish(i):
         groups, _ = steps(i, False)
@@ -1304,9 +1322,13 @@
             shape((n_section, 6, width), F32),
             shape((n_section, n_tensor, 1, 3 * part), F32),
             shape((n_section, n_tensor, 1, span), F32),
+            shape((1, 6, width // (n_dp * n_tensor)), F32),
+            shape((1, part // DH, DH // n_dp), F32),
+            shape((1, part // DH, DH // n_dp), F32),
+            shape((1, span // DH, DH // n_dp), F32),
         ],
         in_specs=[hbm] + [vmem] * 3 + [hbm] * len(saved),
-        out_specs=[hbm] * 3 + [vmem] * 3,
+        out_specs=[hbm] * 3 + [vmem] * 7,
         scratch_shapes=[
             pltpu.VMEM((n_all, n_tensor, width, half), BF16),
             pltpu.VMEM((n_pieces, slots.count, sub, half), BF16),
@@ -1398,7 +1420,7 @@
     gathered, row_out, *kept, vec = gather_and_forward(
         shard, first_rows, live_rows, given, n_section, n_dp, n_tensor
     )
-    weight_sum, sec_rows, sec_grads, d_vec, d_qkv_bias, d_up_bias = backward_and_reduce(
+    weight_sum, sec_rows, sec_grads, _, _, _, vec, q_sum, v_sum, up_sum = backward_and_reduce(
         gathered, own_rows(cotangent), live_rows, vec, [first_rows, row_out, *kept], n_dp
     )
 
@@ -1408,25 +1430,6 @@
 
     section_out = placed_rows(sec_rows)
     input_grad = placed_rows(sec_grads)
-
-    dp_idx, tensor_idx = lax.axis_index("dp"), lax.axis_index("tensor")
-
-    def own_heads(sums, like):
-        _, heads, lanes = like.shape
-        sums = sums.reshape(-1, DH)
-        return lax.dynamic_slice(sums, (0, dp_idx * lanes), (heads, lanes))[None]
-
-    d_vec, d_qkv_bias, d_up_bias = (
-        lax.dynamic_index_in_dim(v, section_idx, 0, keepdims=False)
-        for v in (d_vec, d_qkv_bias, d_up_bias)
-    )
-    q_row, _, v_row = jnp.split(
-        lax.dynamic_index_in_dim(d_qkv_bias, tensor_idx, 0, keepdims=False).reshape(-1), 3
-    )
-    up_row = lax.dynamic_index_in_dim(d_up_bias, tensor_idx, 0, keepdims=False)
-    q_sum, v_sum, up_sum = own_heads(q_row, q_bias), own_heads(v_row, v_bias), own_heads(up_row, up_bias)
-    block = width // (n_dp * n_tensor)
-    vec = lax.dynamic_slice_in_dim(d_vec, (dp_idx * n_tensor + tensor_idx) * block, block, 1)[None]
 
     return (
         section_out,

time: 307 us -> 306 us (level)
    unnamed x27 -> x34, local copies, waits for them, and re-layouts: 7.72 us -> 10.2 us
where the time goes in v3:
time: 306 us; the launch traced here: 309 us
  Pallas kernels  288 us (94%)
  local copies, waits for them, and re-layouts  17.3 us (6%)
    pallas_call x1, Pallas kernels, backward_and_reduce(): pl.pallas_call(functools.partial(backward_kernel, n_dp, n_tensor, images)...  151 us
    pallas_call x1, Pallas kernels, gather_and_forward(): pl.pallas_call(functools.partial(forward_kernel, n_dp, n_tensor, images),...  137 us
    unnamed x34, local copies, waits for them, and re-layouts  10.2 us

profile of v3, /device:TPU:0, one launch (start us, length us, event | category | flops | bytes accessed | tf_op | source)
XLA Modules:
  0.0 308.8 jit_solution(14903965648751595675)
XLA Ops:
  0.6 0.0 copy-start
  0.7 0.0 copy-start.6
  0.7 0.6 copy-done
  1.3 0.1 fusion
  1.4 0.1 broadcast_compare_fusion
  1.5 1.0 copy.39
  2.5 0.9 reshape.65.refs_2_.live
  3.4 0.0 copy-start.4
  3.4 0.0 copy-start.5
  3.4 1.3 copy.38
  4.7 0.2 copy.40
  4.8 0.1 maximum_bitcast_fusion
  4.9 0.0 copy-done.6
  4.9 2.0 pad_maximum_fusion.refs_0_
  6.9 0.0 copy-done.4
  6.9 0.0 copy-done.5
  6.9 1.2 constant_dynamic-slice_fusion
  8.2 0.1 copy.57
  8.3 0.9 pad.14.clone
  9.1 0.1 copy.56
  9.2 0.9 pad.12.clone
  10.1 137.1 %shard_map.231 = (bf16[2,3,4,768,768]{4,3,2,1,0:T(8,128)(2,1)}, bf16[1,416,768]{2,1,0:T(8,128)(2,1)}, bf16[2,4,416,576]{3,2,1,0:T(8,128)(2,1)}, bf16[2,4,2,3,208...) custom-call(bf16[3,192,768]{2,1,0:T(8,128)(2,1)} %pad_maximum_fusion, ...), custom_call_target="tpu_custom_call" | custom-call | tf_op jit(solution)/shard_map/pallas_call | solution.py:618
  147.2 151.2 %shard_map.232 = (f32[3,192,768]{2,1,0:T(8,128)}, bf16[2,416,768]{2,1,0:T(8,128)(2,1)}, bf16[2,416,768]{2,1,0:T(8,128)(2,1)}, f32[2,6,768]{2,1,0:T(8,128)}, f32[...) custom-call(bf16[2,3,4,768,768]{4,3,2,1,0:T(8,128)(2,1)} %get-tuple-, ...), custom_call_target="tpu_custom_call" | custom-call | tf_op jit(solution)/shard_map/pallas_call | solution.py:1316
  298.4 1.4 slice.24
  299.8 0.0 copy-start.3
  299.8 1.5 copy.61
  301.3 0.0 copy-done.3
  301.3 0.1 slice.25
  301.4 0.0 copy-start.10
  301.4 0.0 copy-start.9
  301.4 0.0 copy-start.8
  301.4 0.0 copy-start.7
  301.4 0.0 copy-start.2
  301.4 1.5 copy.60
  302.9 0.0 copy-done.10
  302.9 0.6 copy.50
  303.5 0.0 copy-done.9
  303.5 0.6 copy.51
  304.0 0.0 copy-done.8
  304.0 0.6 copy.53
  304.6 0.0 copy-done.7
  304.6 0.6 copy.52
  305.2 0.0 copy-done.2
  305.2 0.1 slice_bitcast_fusion.1
  305.3 0.8 copy.49
  306.2 0.0 copy-start.1
  306.2 1.1 slice_bitcast_fusion
  307.3 0.2 copy.47
  307.5 1.1 copy.48
  308.6 0.0 copy-done.1
  (3 shorter events, 0.1 us)
Async XLA Ops:
  0.6 0.7 copy-start
  0.7 4.3 %copy-start.6 = (bf16[1,768,192]{1,2,0:T(8,128)(2,1)S(1)}, bf16[1,768,192]{1,2,0:T(8,128)(2,1)}, u32[]{:S(2)}) copy-start(bf16[1,768,192]{1,2,0:T(8,128)(2,1)} %param.30) | copy-start | bytes 884740
  3.4 3.6 %copy-start.4 = (bf16[4,197,768]{2,0,1:T(4,128)(2,1)S(1)}, bf16[4,197,768]{2,0,1:T(4,128)(2,1)}, u32[]{:S(2)}) copy-start(bf16[4,197,768]{2,0,1:T(4,128)(2,1)} %param.17) | copy-start | bytes 3631108
  3.4 3.6 %copy-start.5 = (bf16[4,197,768]{2,0,1:T(4,128)(2,1)S(1)}, bf16[4,197,768]{2,0,1:T(4,128)(2,1)}, u32[]{:S(2)}) copy-start(bf16[4,197,768]{2,0,1:T(4,128)(2,1)} %param.16) | copy-start | bytes 3631108
  299.8 1.5 copy-start.3
  301.4 1.5 copy-start.10
  301.4 2.1 copy-start.9
  301.4 2.7 copy-start.8
  301.4 3.2 %copy-start.7 = (f32[1,12,16]{2,1,0:T(8,128)S(1)}, f32[1,12,16]{2,1,0:T(8,128)}, u32[]{:S(2)}) copy-start(f32[1,12,16]{2,1,0:T(8,128)} %get-tuple-element.60) | copy-start | bytes 2308
  301.4 3.8 %copy-start.2 = (f32[3,192,768]{2,1,0:T(8,128)S(1)}, f32[3,192,768]{2,1,0:T(8,128)}, u32[]{:S(2)}) copy-start(f32[3,192,768]{2,1,0:T(8,128)} %get-tuple-element.37) | copy-start | bytes 5308420
  306.2 2.4 copy-start.1

commit v4 on v3

--- a/solution.py
+++ b/solution.py
@@ -150,7 +150,7 @@
 
 def forward_kernel(n_dp, n_tensor, images, *refs):
     (
-        shard, rows, live, *given,
+        attn_shard, up_shard, down_shard, rows, live, *given,
         out, row_out, qkv_out, p_out, heads_out, middle_out, active_out, slope_out, vec,
         w_buf, qkv_st, p_st, heads_st, active_st, slope_st, middle_st, normed, acc, row_buf,
         qkv_bias, up_bias, vec_in, qkv_bias_in, up_bias_in,
@@ -158,7 +158,9 @@
     ) = refs
     at = Place(n_dp, n_tensor)
     n_section = out.shape[0]
-    n_blk, depth, span = shard.shape
+    shards = (attn_shard, up_shard, down_shard)
+    n_blk = len(shards)
+    depth, span = up_shard.shape
     half = span // 2
     n_all = n_section * n_blk
     n_sub = sub_blocks(depth)
@@ -200,7 +202,7 @@
 
     def share(b):
         return pltpu.make_async_remote_copy(
-            src_ref=shard.at[b],
+            src_ref=shards[b],
             dst_ref=whole(at.s, b),
             send_sem=own_sem.at[1, b],
             recv_sem=own_sem.at[2, b],
@@ -209,7 +211,7 @@
         )
 
     for b in range(n_blk):
-        pltpu.make_async_copy(shard.at[b], whole(at.s, b), own_sem.at[0, b]).start()
+        pltpu.make_async_copy(shards[b], whole(at.s, b), own_sem.at[0, b]).start()
         share(b).start()
 
     def push(i, e, tt, device, e_there, slot, start):
@@ -279,12 +281,12 @@
 
                 @pl.when(jnp.logical_and(sec == at.s, is_first))
                 def _():
-                    pltpu.make_async_copy(shard.at[b], whole(at.s, b), own_sem.at[0, b]).wait()
+                    pltpu.make_async_copy(whole(at.s, b), whole(at.s, b), own_sem.at[0, b]).wait()
 
                 @pl.when(jnp.logical_and(sec != at.s, is_first))
                 def _():
                     pltpu.make_async_remote_copy(
-                        src_ref=shard.at[b],
+                        src_ref=whole(1 - at.s, b),
                         dst_ref=whole(1 - at.s, b),
                         send_sem=own_sem.at[1, b],
                         recv_sem=own_sem.at[2, b],
@@ -601,8 +603,9 @@
     return [known[g] if g < len(known) else known[-1] + 3 * (g - len(known) + 1) for g in range(n_groups)]
 
 
-def gather_and_forward(shard, rows, live, given, n_section, n_dp, n_tensor):
-    n_blk, depth, span = shard.shape
+def gather_and_forward(shards, rows, live, given, n_section, n_dp, n_tensor):
+    n_blk = len(shards)
+    depth, span = shards[1].shape
     n_rows, width = rows.shape
     images = n_rows // ROWS
     part = width // n_tensor
@@ -628,7 +631,7 @@
             shape((n_section, n_tensor, n_rows, span), BF16),
             shape((n_section, 6, width), F32),
         ],
-        in_specs=[hbm] + [vmem] * (2 + len(given)),
+        in_specs=[hbm] * n_blk + [vmem] * (2 + len(given)),
         out_specs=[hbm] * 8 + [vmem],
         scratch_shapes=[
             pltpu.VMEM((2, width, span), BF16),
@@ -659,7 +662,7 @@
         compiler_params=pltpu.CompilerParams(
             collective_id=0, has_side_effects=True, vmem_limit_bytes=56 * 1024 * 1024
         ),
-    )(shard, rows, live, *given)
+    )(*shards, rows, live, *given)
 
 
 class Slots:
@@ -1408,17 +1411,15 @@
     live_rows = live_rows.reshape(-1, SEQ)
     live_rows = jnp.pad(live_rows, ((0, 0), (0, ROWS - SEQ))).reshape(-1, 1)
 
-    shard = jnp.stack(
-        [
-            jnp.concatenate([qkv_weight[0].reshape(depth, -1), out_weight[0].T], axis=1),
-            up_weight[0],
-            down_weight[0].T,
-        ]
+    weight_shards = (
+        jnp.concatenate([qkv_weight[0].reshape(depth, -1), out_weight[0].T], axis=1),
+        up_weight[0],
+        down_weight[0].T,
     )
     given = [ln1_gain, ln1_bias, out_bias, ln2_gain, ln2_bias, down_bias, q_bias, v_bias, up_bias]
     first_rows = own_rows(images)
     gathered, row_out, *kept, vec = gather_and_forward(
-        shard, first_rows, live_rows, given, n_section, n_dp, n_tensor
+        weight_shards, first_rows, live_rows, given, n_section, n_dp, n_tensor
     )
     weight_sum, sec_rows, sec_grads, _, _, _, vec, q_sum, v_sum, up_sum = backward_and_reduce(
         gathered, own_rows(cotangent), live_rows, vec, [first_rows, row_out, *kept], n_dp

time: 306 us -> 297 us (0.971); the launches traced: 309 us -> 296 us
  Pallas kernels: 288 us -> 276 us
    pallas_call x1, Pallas kernels: 151 us -> 139 us  [backward_and_reduce(): pl.pallas_call(functools.partial(backward_kernel, n_dp, n_tensor, images)...]
    unnamed x34 -> x30, local copies, waits for them, and re-layouts: 10.2 us -> 10.1 us
where the time goes in v4:
time: 297 us; the launch traced here: 296 us
  Pallas kernels  276 us (93%)
  local copies, waits for them, and re-layouts  18.5 us (6%)
    pallas_call x1, Pallas kernels, backward_and_reduce(): pl.pallas_call(functools.partial(backward_kernel, n_dp, n_tensor, images)...  139 us
    pallas_call x1, Pallas kernels, gather_and_forward(): pl.pallas_call(functools.partial(forward_kernel, n_dp, n_tensor, images),...  137 us
    unnamed x30, local copies, waits for them, and re-layouts  10.1 us

profile of v4, /device:TPU:0, one launch (start us, length us, event | category | flops | bytes accessed | tf_op | source)
XLA Modules:
  0.0 296.5 jit_solution(12783882964999904628)
XLA Ops:
  0.6 0.0 copy-start
  0.7 0.0 copy-start.4
  0.7 0.6 copy-done
  1.3 0.1 fusion
  1.4 0.1 broadcast_compare_fusion
  1.5 1.0 copy.39
  2.5 0.9 reshape.65.refs_4_.live
  3.4 1.1 copy.38
  4.5 0.2 copy.40
  4.7 0.8 pad_maximum_fusion.refs_0_
  5.5 0.0 copy-done.4
  5.5 2.6 constant_dynamic-slice_fusion
  8.1 0.1 copy.57
  8.2 0.9 pad.14.clone
  9.1 0.1 copy.56
  9.1 0.9 pad.12.clone
  10.0 137.2 %shard_map.231 = (bf16[2,3,4,768,768]{4,3,2,1,0:T(8,128)(2,1)}, bf16[1,416,768]{2,1,0:T(8,128)(2,1)}, bf16[2,4,416,576]{3,2,1,0:T(8,128)(2,1)}, bf16[2,4,2,3,208...) custom-call(bf16[192,768]{1,0:T(8,128)(2,1)} %pad_maximum_fusion.ref, ...), custom_call_target="tpu_custom_call" | custom-call | tf_op jit(solution)/shard_map/pallas_call | solution.py:621
  147.2 139.1 %shard_map.232 = (f32[3,192,768]{2,1,0:T(8,128)}, bf16[2,416,768]{2,1,0:T(8,128)(2,1)}, bf16[2,416,768]{2,1,0:T(8,128)(2,1)}, f32[2,6,768]{2,1,0:T(8,128)}, f32[...) custom-call(bf16[2,3,4,768,768]{4,3,2,1,0:T(8,128)(2,1)} %get-tuple-, ...), custom_call_target="tpu_custom_call" | custom-call | tf_op jit(solution)/shard_map/pallas_call | solution.py:1319
  286.3 1.4 slice.24
  287.7 0.0 copy-start.3
  287.7 1.5 copy.61
  289.2 0.0 copy-done.3
  289.2 0.1 slice.25
  289.3 0.0 copy-start.8
  289.3 0.0 copy-start.7
  289.3 0.0 copy-start.6
  289.3 0.0 copy-start.5
  289.3 0.0 copy-start.2
  289.3 1.5 copy.60
  290.8 0.0 copy-done.8
  290.8 0.6 copy.50
  291.4 0.0 copy-done.7
  291.4 0.6 copy.51
  291.9 0.0 copy-done.6
  292.0 0.6 copy.53
  292.5 0.0 copy-done.5
  292.5 0.6 copy.52
  293.1 0.0 copy-done.2
  293.1 0.1 slice_bitcast_fusion.1
  293.3 0.8 copy.49
  294.1 0.0 copy-start.1
  294.1 1.1 slice_bitcast_fusion
  295.2 0.2 copy.47
  295.4 1.1 copy.48
  296.5 0.0 copy-done.1
  (3 shorter events, 0.1 us)
Async XLA Ops:
  0.6 0.7 copy-start
  0.7 4.8 %copy-start.4 = (bf16[4,197,768]{2,0,1:T(4,128)(2,1)S(1)}, bf16[4,197,768]{2,0,1:T(4,128)(2,1)}, u32[]{:S(2)}) copy-start(bf16[4,197,768]{2,0,1:T(4,128)(2,1)} %param.17) | copy-start | bytes 3631108
  287.7 1.5 copy-start.3
  289.3 1.5 copy-start.8
  289.3 2.1 copy-start.7
  289.3 2.7 copy-start.6
  289.3 3.2 %copy-start.5 = (f32[1,12,16]{2,1,0:T(8,128)S(1)}, f32[1,12,16]{2,1,0:T(8,128)}, u32[]{:S(2)}) copy-start(f32[1,12,16]{2,1,0:T(8,128)} %get-tuple-element.60) | copy-start | bytes 2308
  289.3 3.8 %copy-start.2 = (f32[3,192,768]{2,1,0:T(8,128)S(1)}, f32[3,192,768]{2,1,0:T(8,128)}, u32[]{:S(2)}) copy-start(f32[3,192,768]{2,1,0:T(8,128)} %get-tuple-element.37) | copy-start | bytes 5308420
  294.1 2.4 copy-start.1
